TPU v7x, 128 devices: a whole 4x4x4 slice. The times are simulated.
128 devices in a mesh: dp: 16 (over x, y), tensor: 8 (over z, core).
Axes of the slice: x: 4, y: 4, z: 4, core: 2. Of those that a mesh axis runs over, the one named last changes fastest.
Arguments:
- grad_partial: bfloat16 [8, 32, 1024, 1024], P('tensor', None, 'dp'), may hold values from -0.0625 to 0.0625
- slot_of_block: int32 [32], replicated, may hold values from 0 to 63, as said below
- left_factor: float32 [64, 1024, 1024], P('dp', 'tensor'), as said below
- right_factor: float32 [64, 1024, 1024], P('dp', 'tensor'), as said below
- left_basis: bfloat16 [64, 1024, 1024], P('dp', 'tensor'), may hold values from -0.1875 to 0.1875
- right_basis: bfloat16 [64, 1024, 1024], P('dp', None, 'tensor'), may hold values from -0.1875 to 0.1875
- first_moment: float32 [64, 1024, 1024], P('dp', None, 'tensor'), may hold values from -0.1875 to 0.1875
- second_moment: float32 [64, 1024, 1024], P('dp', None, 'tensor'), as said below
Outputs:
- update: bfloat16 [32, 1024, 1024], P(None, 'dp', 'tensor')
- new_left: float32 [64, 1024, 1024], P('dp', 'tensor')
- new_right: float32 [64, 1024, 1024], P('dp', 'tensor')
- new_first: float32 [64, 1024, 1024], P('dp', None, 'tensor')
- new_second: float32 [64, 1024, 1024], P('dp', None, 'tensor')
Inputs may be any that keep to these rules, and one draw needn't show every extreme that they name: All entries differ; the owner of block b is slot_of_block[b] // 4; some owner holds exactly 4 blocks. `left_factor`: symmetric. `right_factor`: symmetric. `second_moment`: positive.
All inputs are finite; a program needn't handle non-finite values.
Results may differ from a plain program's by a relative error of at most 0.022.
Values may be sent and summed in bfloat16 or wider, within the bound.
A program may use at most 128 MiB of HBM per device.

v0:
```python
import jax
import jax.numpy as jnp
from jax import lax
from jax.sharding import PartitionSpec as P

first_beta = 0.9
second_beta = 0.95
epsilon = 1e-08


def per_device(
    grad_partial,
    slot_of_block,
    left_factor,
    right_factor,
    left_basis,
    right_basis,
    first_moment,
    second_moment,
):
    local_part = grad_partial[0]
    block_count = local_part.shape[0]
    dp_rows = local_part.shape[1]
    owned_slots = left_factor.shape[0]
    slab_width = left_factor.shape[1]
    owner_count = lax.axis_size("dp")
    slot_ids = jnp.arange(owner_count * owned_slots, dtype=jnp.int32)
    take_slot = (slot_of_block[:, None] == slot_ids[None, :]).astype(jnp.bfloat16)
    take_owner = take_slot.reshape(block_count, owner_count, owned_slots)
    outgoing = jnp.einsum(
        "boc,brk->cork", take_owner, local_part, preferred_element_type=jnp.float32
    ).astype(jnp.bfloat16)
    outgoing = outgoing.reshape(owned_slots, owner_count * dp_rows, local_part.shape[2])
    incoming = lax.all_to_all(outgoing, "dp", split_axis=1, concat_axis=1, tiled=True)
    grad_slots = lax.psum_scatter(
        incoming.astype(jnp.float32).astype(jnp.bfloat16), "tensor", scatter_dimension=2, tiled=True
    )
    full_grad, full_left = (
        lax.all_gather(grad_slots, "tensor", axis=2, tiled=True),
        lax.all_gather(left_basis, "tensor", axis=1, tiled=True),
    )
    row_start = lax.axis_index("tensor") * slab_width
    grad_band = lax.dynamic_slice_in_dim(full_grad, row_start, slab_width, 1)
    outer_left = jnp.einsum(
        "jrk,jck->jrc", grad_band, full_grad, preferred_element_type=jnp.float32
    )
    outer_right = jnp.einsum(
        "jkr,jkc->jrc", grad_slots, full_grad, preferred_element_type=jnp.float32
    )
    new_left = second_beta * left_factor + (1.0 - second_beta) * outer_left
    new_right = second_beta * right_factor + (1.0 - second_beta) * outer_right
    rotated = jnp.einsum(
        "jak,jkr->jar", full_grad, right_basis, preferred_element_type=jnp.float32
    ).astype(jnp.bfloat16)
    eigen_grad = jnp.einsum("jak,jkr->jar", full_left, rotated, preferred_element_type=jnp.float32)
    new_first = first_beta * first_moment + (1.0 - first_beta) * eigen_grad
    new_second = second_beta * second_moment + (1.0 - second_beta) * eigen_grad * eigen_grad
    normed = (new_first / (jnp.sqrt(new_second) + epsilon)).astype(jnp.bfloat16)
    back = jnp.einsum("jka,jkr->jar", full_left, normed, preferred_element_type=jnp.float32).astype(
        jnp.bfloat16
    )
    update_cols = lax.psum_scatter(
        jnp.einsum("jar,jcr->cja", back, right_basis, preferred_element_type=jnp.float32).astype(
            jnp.bfloat16
        ),
        "tensor",
        scatter_dimension=0,
        tiled=True,
    )
    returned = lax.all_to_all(update_cols, "dp", split_axis=2, concat_axis=1, tiled=True)
    update = jnp.einsum(
        "bs,ksr->brk", take_slot, returned, preferred_element_type=jnp.float32
    ).astype(jnp.bfloat16)
    return (update, new_left, new_right, new_first, new_second)


def solution(mesh):
    in_specs = (
        P("tensor", None, "dp", None),
        P(),
        P("dp", "tensor", None),
        P("dp", "tensor", None),
        P("dp", "tensor", None),
        P("dp", None, "tensor"),
        P("dp", None, "tensor"),
        P("dp", None, "tensor"),
    )
    out_specs = (
        P(None, "dp", "tensor"),
        P("dp", "tensor", None),
        P("dp", "tensor", None),
        P("dp", None, "tensor"),
        P("dp", None, "tensor"),
    )
    return jax.shard_map(
        per_device, mesh=mesh, in_specs=in_specs, out_specs=out_specs, check_vma=False
    )
```

profile of v0, /device:TPU:1, one launch (start us, length us, event | category | flops | bytes accessed | tf_op | source)
XLA Modules:
  0.0 460.0 jit_solution(7996689162938504899)
XLA Ops:
  7.2 0.0 copy-start
  7.2 0.0 reduce-scatter.7.cloned.1.call-start
  7.2 11.9 %convert_bitcast_fusion = bf16[4,16,64,1024]{3,1,2,0:T(8,128)(2,1)} fusion(bf16[32,64,1024]{2,1,0:T(8,128)(2,1)} %bitcast.52, s32[16,4]{0,1:T(4,128)S(1)} %multiply_add_fusion.2, s32[32]{0:T(128)} %param.9), kind=kOutput, calls=%fused_computation | convolution fusion | flops 272631808 | bytes 12583296 | tf_op jit(solution)/shard_map/boc,brk->cork/dot_general | solution.py:30
  19.2 11.4 %copy.32 = bf16[4,16,64,1024]{3,2,1,0:T(8,128)(2,1)} copy(bf16[4,16,64,1024]{3,1,2,0:T(8,128)(2,1)} %convert_bitcast_fusion) | data formatting | bytes 16777216 | tf_op jit(solution)/shard_map/convert_element_type | solution.py:32
  30.6 10.1 %copy.33 = bf16[4,1024,1024]{2,0,1:T(4,128)(2,1)S(1)} copy(bf16[4,1024,1024]{2,1,0:T(8,128)(2,1)} %bitcast.45) | data formatting | bytes 16777216 | tf_op jit(solution)/shard_map/reshape | solution.py:33
  40.7 102.2 %all_to_all.23 = bf16[4,1024,1024]{2,0,1:T(4,128)(2,1)} all-to-all(bf16[4,1024,1024]{2,0,1:T(4,128)(2,1)S(1)} %copy.33), channel_id=1, replica_groups=mesh['dp'=16,'tensor'=8] {'dp'}, dimensions={1} | all-to-all | bytes 16777216 | tf_op jit(solution)/shard_map/all_to_all | solution.py:34
  142.9 18.8 %copy.48 = bf16[4,1024,1024]{1,0,2:T(4,128)(2,1)} copy(bf16[4,1024,1024]{2,0,1:T(4,128)(2,1)} %all_to_all.23) | data formatting | bytes 16777216
  161.8 12.1 %copy.55 = bf16[128,8,4,1024]{3,1,2,0:T(8,128)(2,1)} copy(bf16[128,8,4,1024]{3,2,1,0:T(4,128)(2,1)} %bitcast.46) | data formatting | bytes 16777216
  173.9 0.0 reduce-scatter.7.cloned.1.call-update
  173.9 0.0 all-gather.5.cloned.1.call-start
  173.9 0.7 all-gather.5.cloned.1.call-update
  174.7 0.0 all-gather.3.cloned.1.call-start
  174.7 52.8 %reduce-scatter.7.cloned.1.call-done = bf16[128,4096]{1,0:T(8,128)(2,1)} async-done(((bf16[1024,4096]{1,0:T(8,128)(2,1)}), bf16[128,4096]{1,0:T(8,128)(2,1)}) %reduce-scatter.7.cloned.1.call-update) | async-done | bytes 1048592
  227.5 1.8 reshape.37
  229.3 1.7 copy.49
  231.0 0.0 all-gather.3.cloned.1.call-update
  231.0 0.0 copy-start.2
  231.0 0.3 reduce-scatter.9.cloned.1.call-start
  231.3 3.0 copy.30
  234.3 0.0 copy-done.2
  234.3 1.8 copy.36
  236.2 43.6 %all-gather.5.cloned.1.call-done = bf16[4,1024,1024]{2,1,0:T(8,128)(2,1)} async-done(((bf16[4,128,1024]{2,1,0:T(8,128)(2,1)}), bf16[4,1024,1024]{2,1,0:T(8,128)(2,1)}) %all-gather.5.cloned.1.call-update) | async-done | bytes 8388624 | tf_op jit(solution)/shard_map/all_gather | solution.py:40
  279.7 56.5 %all-gather.3.cloned.1.call-done = bf16[4,1024,1024]{2,1,0:T(8,128)(2,1)} async-done(((bf16[4,1024,128]{2,1,0:T(8,128)(2,1)}), bf16[4,1024,1024]{2,1,0:T(8,128)(2,1)}) %all-gather.3.cloned.1.call-update) | async-done | bytes 8388624 | tf_op jit(solution)/shard_map/all_gather | solution.py:39
  336.2 0.0 copy-done
  336.2 13.6 %fusion.2 = (f32[4,1024,128]{1,2,0:T(8,128)S(1)}, f32[4,1024,128]{1,2,0:T(8,128)}) fusion(f32[4,1024,128]{1,2,0:T(8,128)} %copy.36, f32[4,1024,128]{1,2,0:T(8,128)} %copy.30, bf16[4,1024,1024]{2,1,0:T(8,128)(2,1)} %all-gather.5.cloned.1.call-done, bf16[4,1024,1024]{2,1,0:T(8,128)(2,1)} %all-gather.3.cloned.1.call-done, bf16[4,1024,128]{2,1,0:T(8,128)(2,1)S(1)} %copy-done), kind=kOutput, calls=%fused_computation.5 | convolution fusion | flops 2151677952 | bytes 26214400 | tf_op jit(solution)/shard_map/jak,jkr->jar/dot_general | solution.py:55
  349.8 12.2 %convolution_convert_fusion = bf16[4,1024,1024]{2,1,0:T(8,128)(2,1)} fusion(bf16[4,1024,128]{2,1,0:T(8,128)(2,1)S(1)} %copy-done, bf16[4,1024,1024]{2,1,0:T(8,128)(2,1)} %all-gather.5.cloned.1.call-done, f32[4,1024,128]{1,2,0:T(8,128)} %get-tuple-element.21, f32[4,1024,128]{1,2,0:T(8,128)S(1)} %get-tuple-element.20), kind=kOutput, calls=%fused_computation.1 | convolution fusion | flops 2153775104 | bytes 22020096 | tf_op jit(solution)/shard_map/jar,jcr->cja/dot_general | solution.py:63
  361.9 11.8 %copy.53 = bf16[1024,4096]{1,0:T(8,128)(2,1)} copy(bf16[1024,4096]{0,1:T(8,128)(2,1)} %bitcast.47) | data formatting | bytes 16777216
  373.7 0.0 reduce-scatter.9.cloned.1.call-update
  373.7 2.9 copy.42
  376.6 1.8 copy.43
  378.4 47.8 %reduce-scatter.9.cloned.1.call-done = bf16[128,4096]{1,0:T(8,128)(2,1)} async-done(((bf16[1024,4096]{1,0:T(8,128)(2,1)}), bf16[128,4096]{1,0:T(8,128)(2,1)}) %reduce-scatter.9.cloned.1.call-update) | async-done | bytes 1048592
  426.2 1.6 copy.54
  427.8 1.9 copy.38
  429.7 6.5 %all-to-all-start.1 = ((bf16[128,4,1024]{0,1,2:T(4,128)(2,1)}), bf16[128,4,1024]{0,1,2:T(4,128)(2,1)S(1)}, u32[]{:S(2)}, u32[]{:S(2)}) async-start(bf16[128,4,1024]{0,1,2:T(4,128)(2,1)} %copy.38), calls=%async_computation.1 | async-start | bytes 2097152 | tf_op jit(solution)/shard_map/all_to_all | solution.py:70
  436.2 0.0 copy-start.1
  436.2 0.0 copy-start.3
  436.2 8.7 %multiply_add_fusion.1 = f32[4,128,1024]{2,1,0:T(8,128)} fusion(f32[4,128,1024]{2,1,0:T(8,128)} %param.10, bf16[4,1024,1024]{2,1,0:T(8,128)(2,1)} %all-gather.3.cloned.1.call-done, s32[]{:T(128)S(6)} %select_n.3), kind=kOutput, calls=%fused_computation.9 | convolution fusion | flops 1075314688 | bytes 13631492 | tf_op jit(solution)/shard_map/jrk,jck->jrc/dot_general | solution.py:44
  445.0 0.0 copy-done.1
  445.0 0.0 copy-done.3
  445.0 6.5 %multiply_add_fusion = f32[4,128,1024]{2,1,0:T(8,128)} fusion(f32[4,128,1024]{2,1,0:T(8,128)S(1)} %copy-done.3, bf16[4,1024,128]{2,1,0:T(8,128)(2,1)S(1)} %copy-done.1, bf16[4,1024,1024]{2,1,0:T(8,128)(2,1)} %all-gather.3.cloned.1.call-done), kind=kOutput, calls=%fused_computation.8 | convolution fusion | flops 1075314688 | bytes 13631488 | tf_op jit(solution)/shard_map/jkr,jkc->jrc/dot_general | solution.py:47
  451.5 0.0 copy-start.4
  451.5 0.0 all-to-all-done.1
  451.5 0.6 copy.39
  452.0 0.1 copy-done.4
  452.1 0.3 fusion.4
  452.5 1.0 copy.41
  (1 shorter events, 0.0 us)
Async XLA Ops:
  7.2 329.0 %copy-start = (bf16[4,1024,128]{2,1,0:T(8,128)(2,1)S(1)}, bf16[4,1024,128]{2,1,0:T(8,128)(2,1)}, u32[]{:S(2)}) copy-start(bf16[4,1024,128]{2,1,0:T(8,128)(2,1)} %param.13) | copy-start | bytes 3145732
  7.2 220.3 %reduce-scatter.7.cloned.1.call-start = ((), (), s32[]{:S(2)}) async-start(), calls=%async_computation.6 | async-start | bytes 9437184
  173.9 105.8 %all-gather.5.cloned.1.call-start = ((), (), s32[]{:S(2)}) async-start(), calls=%async_computation.5 | async-start | bytes 9437184 | tf_op jit(solution)/shard_map/all_gather | solution.py:40
  174.7 161.5 %all-gather.3.cloned.1.call-start = ((), (), s32[]{:S(2)}) async-start(), calls=%async_computation.4 | async-start | bytes 9437184 | tf_op jit(solution)/shard_map/all_gather | solution.py:39
  231.0 3.3 copy-start.2
  231.0 195.1 %reduce-scatter.9.cloned.1.call-start = ((), (), s32[]{:S(2)}) async-start(), calls=%async_computation.7 | async-start | bytes 9437184
  429.7 21.8 %all-to-all-start.1 = ((bf16[128,4,1024]{0,1,2:T(4,128)(2,1)}), bf16[128,4,1024]{0,1,2:T(4,128)(2,1)S(1)}, u32[]{:S(2)}, u32[]{:S(2)}) async-start(bf16[128,4,1024]{0,1,2:T(4,128)(2,1)} %copy.38), calls=%async_computation.1 | async-start | bytes 2097152 | tf_op jit(solution)/shard_map/all_to_all | solution.py:70
  436.2 8.8 %copy-start.1 = (bf16[4,1024,128]{2,1,0:T(8,128)(2,1)S(1)}, bf16[4,1024,128]{2,1,0:T(8,128)(2,1)}, u32[]{:S(2)}) copy-start(bf16[4,1024,128]{2,1,0:T(8,128)(2,1)} %copy.49) | copy-start | bytes 3145732
  436.2 8.8 %copy-start.3 = (f32[4,128,1024]{2,1,0:T(8,128)S(1)}, f32[4,128,1024]{2,1,0:T(8,128)}, u32[]{:S(2)}) copy-start(f32[4,128,1024]{2,1,0:T(8,128)} %param.11) | copy-start | bytes 6291460
  451.5 0.7 copy-start.4
Sparse Core Ops, SparseCore 0:
  174.0 53.3 reduce-scatter.6
  229.1 50.5 all-gather.4
  282.0 54.1 all-gather.2
  373.8 52.2 reduce-scatter.8
where the time goes:
time: 463 us; the launch traced here: 460 us
  waiting for transfers between devices  201 us (43%)
  blocking collectives  102 us (22%)
  local copies, waits for them, and re-layouts  82.5 us (18%)
  matrix products  53.2 us (11%)
  between operations  13.9 us (3%)
  starting transfers between devices  6.91 us (1%)
    all_to_all x1, blocking collectives, per_device(): lax.all_to_all(outgoing, 'dp', split_axis=1, concat_axis=1, tiled=True)  102 us
    unnamed x6, waiting for transfers between devices  101 us
    unnamed x21, local copies, waits for them, and re-layouts  58.5 us
    all_gather x1, waiting for transfers between devices, per_device(): lax.all_gather(grad_slots, 'tensor', axis=2, tiled=True)  56.5 us
    all_gather x1, waiting for transfers between devices, per_device(): lax.all_gather(left_basis, 'tensor', axis=1, tiled=True)  43.6 us
    dot_general x1, matrix products, per_device(): jnp.einsum('jak,jkr->jar', full_left, rotated, preferred_element_type=jnp...  13.6 us
    dot_general x1, matrix products, per_device(): jnp.einsum('jar,jcr->cja', back, right_basis, preferred_element_type=jnp....  12.2 us
    dot_general x1, matrix products, per_device(): jnp.einsum('boc,brk->cork', take_owner, local_part, preferred_element_typ...  11.9 us
  transfers between devices with their start and end apart: 5, of which 4 were waited for; matrix products, arithmetic and copies ran while one was open for 6% of the time, Pallas kernels for 0%

commit v1 on v0

--- a/solution.py
+++ b/solution.py
@@ -26,14 +26,14 @@
     owner_count = lax.axis_size("dp")
     slot_ids = jnp.arange(owner_count * owned_slots, dtype=jnp.int32)
     take_slot = (slot_of_block[:, None] == slot_ids[None, :]).astype(jnp.bfloat16)
-    take_owner = take_slot.reshape(block_count, owner_count, owned_slots)
+    summed = lax.psum_scatter(local_part, "tensor", scatter_dimension=2, tiled=True)
     outgoing = jnp.einsum(
-        "boc,brk->cork", take_owner, local_part, preferred_element_type=jnp.float32
+        "bs,brc->src", take_slot, summed, preferred_element_type=jnp.float32
     ).astype(jnp.bfloat16)
-    outgoing = outgoing.reshape(owned_slots, owner_count * dp_rows, local_part.shape[2])
-    incoming = lax.all_to_all(outgoing, "dp", split_axis=1, concat_axis=1, tiled=True)
-    grad_slots = lax.psum_scatter(
-        incoming.astype(jnp.float32).astype(jnp.bfloat16), "tensor", scatter_dimension=2, tiled=True
+    outgoing = outgoing.reshape(owner_count, owned_slots, dp_rows, slab_width)
+    incoming = lax.all_to_all(outgoing, "dp", split_axis=0, concat_axis=0, tiled=True)
+    grad_slots = incoming.transpose(1, 0, 2, 3).reshape(
+        owned_slots, owner_count * dp_rows, slab_width
     )
     full_grad, full_left = (
         lax.all_gather(grad_slots, "tensor", axis=2, tiled=True),

time: 463 us -> 307 us (0.66)
  blocking collectives: 102 us -> 19.5 us
  waiting for transfers between devices: 201 us -> 166 us
  local copies, waits for them, and re-layouts: 82.5 us -> 57 us
  matrix products: 53.2 us -> 40.7 us
    all_to_all x1, blocking collectives: 102 us -> 19.5 us  [per_device(): lax.all_to_all(outgoing, 'dp', split_axis=0, concat_axis=0, tiled=True)]
    all_gather x1, waiting for transfers between devices: 43.6 us -> 23 us  [per_device(): lax.all_gather(left_basis, 'tensor', axis=1, tiled=True)]
    unnamed x6, waiting for transfers between devices: 101 us -> 86.3 us
    convert_element_type x1 -> x0, local copies, waits for them, and re-layouts: 11.4 us -> none  [per_device(): outgoing = jnp.einsum('boc,brk->cork', take_owner, local_part, preferred_...]
    dot_general x1, matrix products: 11.9 us -> 0.55 us  [per_device(): jnp.einsum('bs,brc->src', take_slot, summed, preferred_element_type=jnp.f...]
    reshape x1, local copies, waits for them, and re-layouts: 10.1 us -> 0.48 us  [per_device(): outgoing = outgoing.reshape(owner_count, owned_slots, dp_rows, slab_width)]
    unnamed x21 -> x22, local copies, waits for them, and re-layouts: 58.5 us -> 51.3 us
  transfers between devices with their start and end apart: 5 -> 5, of which waited for: 4 -> 4; matrix products, arithmetic and copies ran while one was open for 6% -> 10% of each run, Pallas kernels for 0% -> 0%
where the time goes in v1:
time: 307 us; the launch traced here: 304 us
  waiting for transfers between devices  166 us (54%)
  local copies, waits for them, and re-layouts  57 us (19%)
  matrix products  40.7 us (13%)
  blocking collectives  19.5 us (6%)
  between operations  13.9 us (5%)
  starting transfers between devices  6.88 us (2%)
    unnamed x6, waiting for transfers between devices  86.3 us
    all_gather x1, waiting for transfers between devices, per_device(): lax.all_gather(grad_slots, 'tensor', axis=2, tiled=True)  56.5 us
    unnamed x22, local copies, waits for them, and re-layouts  51.3 us
    all_gather x1, waiting for transfers between devices, per_device(): lax.all_gather(left_basis, 'tensor', axis=1, tiled=True)  23 us
    all_to_all x1, blocking collectives, per_device(): lax.all_to_all(outgoing, 'dp', split_axis=0, concat_axis=0, tiled=True)  19.5 us
    dot_general x1, matrix products, per_device(): jnp.einsum('jak,jkr->jar', full_left, rotated, preferred_element_type=jnp...  15.1 us
    dot_general x1, matrix products, per_device(): jnp.einsum('jar,jcr->cja', back, right_basis, preferred_element_type=jnp....  9.53 us
    dot_general x1, matrix products, per_device(): jnp.einsum('jrk,jck->jrc', grad_band, full_grad, preferred_element_type=j...  8.74 us
  transfers between devices with their start and end apart: 5, of which 4 were waited for; matrix products, arithmetic and copies ran while one was open for 10% of the time, Pallas kernels for 0%

profile of v1, /device:TPU:1, one launch (start us, length us, event | category | flops | bytes accessed | tf_op | source)
XLA Modules:
  0.0 303.7 jit_solution(12736105989068220977)
XLA Ops:
  7.2 0.0 copy-start
  7.2 0.0 reduce-scatter.7.cloned.1.call-start
  7.2 13.0 %copy.34 = bf16[32,64,1024]{1,0,2:T(8,128)(2,1)} copy(bf16[32,64,1024]{2,1,0:T(8,128)(2,1)} %bitcast.40) | data formatting | bytes 8388608
  20.3 12.3 %reshape.20 = bf16[1024,2048]{1,0:T(8,128)(2,1)} reshape(bf16[1024,32,64]{2,1,0:T(8,128)(2,1)} %bitcast.36) | data formatting | bytes 8388608
  32.6 0.0 reduce-scatter.7.cloned.1.call-update
  32.6 0.0 copy-start.5
  32.6 0.0 all-gather.5.cloned.1.call-start
  32.7 0.7 all-gather.5.cloned.1.call-update
  33.4 0.0 all-gather.3.cloned.1.call-start
  33.4 37.8 %reduce-scatter.7.cloned.1.call-done = bf16[128,2048]{1,0:T(8,128)(2,1)} async-done(((bf16[1024,2048]{1,0:T(8,128)(2,1)}), bf16[128,2048]{1,0:T(8,128)(2,1)}) %reduce-scatter.7.cloned.1.call-update) | async-done | bytes 524304
  71.2 2.1 reshape.21
  73.3 1.5 copy.23
  74.8 0.0 copy-done.5
  74.8 0.5 convolution_convert_fusion.1
  75.4 0.5 copy.24
  75.9 19.5 %all_to_all.23 = bf16[16,4,64,128]{3,1,2,0:T(4,128)(2,1)S(1)} all-to-all(bf16[16,4,64,128]{3,1,2,0:T(4,128)(2,1)S(1)} %copy.24), channel_id=1, replica_groups=mesh['dp'=16,'tensor'=8] {'dp'}, dimensions={0} | all-to-all | bytes 2097152 | tf_op jit(solution)/shard_map/all_to_all | solution.py:34
  95.3 0.0 copy-start.3
  95.3 1.2 copy.25
  96.6 0.0 all-gather.3.cloned.1.call-update
  96.6 0.2 reduce-scatter.9.cloned.1.call-start
  96.8 0.5 copy-done.3
  97.4 1.8 copy.22
  99.2 2.9 copy.26
  102.0 23.0 %all-gather.5.cloned.1.call-done = bf16[4,1024,1024]{2,1,0:T(8,128)(2,1)} async-done(((bf16[4,128,1024]{2,1,0:T(8,128)(2,1)}), bf16[4,1024,1024]{2,1,0:T(8,128)(2,1)}) %all-gather.5.cloned.1.call-update) | async-done | bytes 8388624 | tf_op jit(solution)/shard_map/all_gather | solution.py:40
  125.0 56.5 %all-gather.3.cloned.1.call-done = bf16[4,1024,1024]{2,1,0:T(8,128)(2,1)} async-done(((bf16[4,1024,128]{2,1,0:T(8,128)(2,1)}), bf16[4,1024,1024]{2,1,0:T(8,128)(2,1)}) %all-gather.3.cloned.1.call-update) | async-done | bytes 8388624 | tf_op jit(solution)/shard_map/all_gather | solution.py:39
  181.5 0.0 copy-done
  181.5 15.1 %fusion = (f32[4,1024,128]{1,2,0:T(8,128)S(1)}, f32[4,1024,128]{1,2,0:T(8,128)}) fusion(f32[4,1024,128]{1,2,0:T(8,128)} %copy.26, f32[4,1024,128]{1,2,0:T(8,128)} %copy.22, bf16[4,1024,1024]{2,1,0:T(8,128)(2,1)} %all-gather.5.cloned.1.call-done, bf16[4,1024,1024]{2,1,0:T(8,128)(2,1)} %all-gather.3.cloned.1.call-done, bf16[4,1024,128]{2,1,0:T(8,128)(2,1)S(1)} %copy-done), kind=kOutput, calls=%fused_computation.2 | convolution fusion | flops 2151677952 | bytes 26214400 | tf_op jit(solution)/shard_map/jak,jkr->jar/dot_general | solution.py:55
  196.6 9.5 %convolution_convert_fusion = bf16[4,1024,1024]{2,1,0:T(8,128)(2,1)} fusion(bf16[4,1024,128]{2,1,0:T(8,128)(2,1)S(1)} %copy-done, bf16[4,1024,1024]{2,1,0:T(8,128)(2,1)} %all-gather.5.cloned.1.call-done, f32[4,1024,128]{1,2,0:T(8,128)} %get-tuple-element.16, f32[4,1024,128]{1,2,0:T(8,128)S(1)} %get-tuple-element.15), kind=kOutput, calls=%fused_computation | convolution fusion | flops 2153775104 | bytes 22020096 | tf_op jit(solution)/shard_map/jar,jcr->cja/dot_general | solution.py:63
  206.1 11.3 %copy.39 = bf16[1024,4096]{1,0:T(8,128)(2,1)} copy(bf16[1024,4096]{0,1:T(8,128)(2,1)} %bitcast.37) | data formatting | bytes 16777216
  217.5 0.0 reduce-scatter.9.cloned.1.call-update
  217.5 2.9 copy.31
  220.4 1.8 copy.32
  222.2 47.8 %reduce-scatter.9.cloned.1.call-done = bf16[128,4096]{1,0:T(8,128)(2,1)} async-done(((bf16[1024,4096]{1,0:T(8,128)(2,1)}), bf16[128,4096]{1,0:T(8,128)(2,1)}) %reduce-scatter.9.cloned.1.call-update) | async-done | bytes 1048592
  270.0 1.6 copy.40
  271.6 1.9 copy.27
  273.5 6.5 %all-to-all-start.1 = ((bf16[128,4,1024]{0,1,2:T(4,128)(2,1)}), bf16[128,4,1024]{0,1,2:T(4,128)(2,1)S(1)}, u32[]{:S(2)}, u32[]{:S(2)}) async-start(bf16[128,4,1024]{0,1,2:T(4,128)(2,1)} %copy.27), calls=%async_computation.1 | async-start | bytes 2097152 | tf_op jit(solution)/shard_map/all_to_all | solution.py:70
  280.0 0.0 copy-start.2
  280.0 0.0 copy-start.4
  280.0 8.7 %multiply_add_fusion.1 = f32[4,128,1024]{2,1,0:T(8,128)} fusion(f32[4,128,1024]{2,1,0:T(8,128)} %param.10, bf16[4,1024,1024]{2,1,0:T(8,128)(2,1)} %all-gather.3.cloned.1.call-done, s32[]{:T(128)S(6)} %select_n.3), kind=kOutput, calls=%fused_computation.6 | convolution fusion | flops 1075314688 | bytes 13631492 | tf_op jit(solution)/shard_map/jrk,jck->jrc/dot_general | solution.py:44
  288.8 0.0 copy-done.2
  288.8 0.0 copy-done.4
  288.8 6.4 %multiply_add_fusion = f32[4,128,1024]{2,1,0:T(8,128)} fusion(f32[4,128,1024]{2,1,0:T(8,128)S(1)} %copy-done.4, bf16[4,1024,128]{2,1,0:T(8,128)(2,1)S(1)} %bitcast.39, bf16[4,1024,1024]{2,1,0:T(8,128)(2,1)} %all-gather.3.cloned.1.call-done), kind=kOutput, calls=%fused_computation.5 | convolution fusion | flops 1075314688 | bytes 13631488 | tf_op jit(solution)/shard_map/jkr,jkc->jrc/dot_general | solution.py:47
  295.2 0.0 all-to-all-done.1
  295.2 0.0 copy-start.1
  295.2 0.6 copy.28
  295.8 0.4 fusion.2
  296.2 1.0 copy.30
  297.2 0.0 copy-done.1
Async XLA Ops:
  7.2 174.3 %copy-start = (bf16[4,1024,128]{2,1,0:T(8,128)(2,1)S(1)}, bf16[4,1024,128]{2,1,0:T(8,128)(2,1)}, u32[]{:S(2)}) copy-start(bf16[4,1024,128]{2,1,0:T(8,128)(2,1)} %param.13) | copy-start | bytes 3145732
  7.2 64.0 %reduce-scatter.7.cloned.1.call-start = ((), (), s32[]{:S(2)}) async-start(), calls=%async_computation.6 | async-start | bytes 4718592
  32.6 42.2 %copy-start.5 = (s32[32]{0:T(128)S(1)}, s32[32]{0:T(128)}, u32[]{:S(2)}) copy-start(s32[32]{0:T(128)} %param.9) | copy-start | bytes 388
  32.6 92.4 %all-gather.5.cloned.1.call-start = ((), (), s32[]{:S(2)}) async-start(), calls=%async_computation.5 | async-start | bytes 9437184 | tf_op jit(solution)/shard_map/all_gather | solution.py:40
  33.4 148.1 %all-gather.3.cloned.1.call-start = ((), (), s32[]{:S(2)}) async-start(), calls=%async_computation.4 | async-start | bytes 9437184 | tf_op jit(solution)/shard_map/all_gather | solution.py:39
  95.3 2.0 copy-start.3
  96.6 173.4 %reduce-scatter.9.cloned.1.call-start = ((), (), s32[]{:S(2)}) async-start(), calls=%async_computation.7 | async-start | bytes 9437184
  273.5 21.8 %all-to-all-start.1 = ((bf16[128,4,1024]{0,1,2:T(4,128)(2,1)}), bf16[128,4,1024]{0,1,2:T(4,128)(2,1)S(1)}, u32[]{:S(2)}, u32[]{:S(2)}) async-start(bf16[128,4,1024]{0,1,2:T(4,128)(2,1)} %copy.27), calls=%async_computation.1 | async-start | bytes 2097152 | tf_op jit(solution)/shard_map/all_to_all | solution.py:70
  280.0 8.8 %copy-start.2 = (bf16[4,16,64,128]{3,2,1,0:T(8,128)(2,1)S(1)}, bf16[4,16,64,128]{3,2,1,0:T(8,128)(2,1)}, u32[]{:S(2)}) copy-start(bf16[4,16,64,128]{3,2,1,0:T(8,128)(2,1)} %copy.25) | copy-start | bytes 3145732
  280.0 8.8 %copy-start.4 = (f32[4,128,1024]{2,1,0:T(8,128)S(1)}, f32[4,128,1024]{2,1,0:T(8,128)}, u32[]{:S(2)}) copy-start(f32[4,128,1024]{2,1,0:T(8,128)} %param.11) | copy-start | bytes 6291460
  295.2 1.9 copy-start.1
Sparse Core Ops, SparseCore 0:
  32.7 38.4 reduce-scatter.6
  72.9 52.0 all-gather.4
  127.3 54.1 all-gather.2
  217.6 52.2 reduce-scatter.8

commit v2 on v1

v2 whole, which is shorter than its diff:
```python
import functools
import jax
import jax.numpy as jnp
from jax import lax
from jax.experimental import pallas as pl
from jax.experimental.pallas import tpu as pltpu
from jax.sharding import PartitionSpec as P

first_beta = 0.9
second_beta = 0.95
epsilon = 1e-08
f32 = jnp.float32
bf16 = jnp.bfloat16
CHUNKS = 4


def aligned(index, size):
    return pl.ds(pl.multiple_of(index * size, size), size)


def dot(a, b, dims):
    return lax.dot_general(a, b, (dims, ((), ())), preferred_element_type=f32)


def step_kernel(
    n_dp,
    nz,
    slot_ref,
    inv_ref,
    gp,
    lb,
    rb,
    first_hbm,
    second_hbm,
    upd,
    ein,
    ggt_in,
    gtg_in,
    mine,
    sibr,
    rsr,
    summed,
    stage,
    grad,
    left,
    right,
    rot,
    eig,
    first,
    second,
    nout,
    normed,
    back,
    ggo,
    gto,
    ucols,
    uin,
    load_sem,
    mine_sem,
    sib_ss,
    sib_rs,
    rs_ss,
    rs_rs,
    a_ss,
    a_rs,
    r_ss,
    r_rs,
    l_ss,
    l_rs,
    gg_ss,
    gg_rs,
    gt_ss,
    gt_rs,
    e_ss,
    e_rs,
    n_ss,
    n_rs,
    g_sib_ss,
    g_sib_rs,
    l_sib_ss,
    l_sib_rs,
    b_sib_ss,
    b_sib_rs,
    one_ss,
    one_rs,
):
    blocks, rows, order = gp.shape
    width = lb.shape[1]
    size = order // CHUNKS
    dp = lax.axis_index("dp")
    t = lax.axis_index("tensor")
    z = t // 2
    c = t % 2
    sibling = (dp, 2 * z + 1 - c)
    devices = n_dp * nz

    def peer(o, k):
        return (o, 2 * k + c)

    def send(src, dst, ss, rs, dev):
        copy = pltpu.make_async_remote_copy(
            src_ref=src,
            dst_ref=dst,
            send_sem=ss,
            recv_sem=rs,
            device_id=dev,
            device_id_type=pl.DeviceIdType.MESH,
        )
        copy.start()
        return copy

    def local(src, dst, sem):
        copy = pltpu.make_async_copy(src, dst, sem)
        copy.start()
        return copy

    def plus(i):
        return lax.rem(z + i, nz)

    def minus(i):
        return lax.rem(z + nz - i, nz)

    def partner(i):
        return lax.rem(dp + i // nz, n_dp), lax.rem(z + i % nz, nz)

    load_first = local(first_hbm, first, load_sem.at[0])
    load_second = local(second_hbm, second, load_sem.at[1])
    turns = [i for i in range(1, nz)] + [0]
    mine_copies = {}
    for i in turns:
        mine_copies[i] = local(
            gp.at[:, :, aligned(2 * plus(i) + c, width)], mine.at[i], mine_sem.at[i]
        )

    barrier = pltpu.get_barrier_semaphore()

    @pl.loop(1, devices)
    def _(i):
        o, k = partner(i)
        pl.semaphore_signal(
            barrier, inc=1, device_id=peer(o, k), device_id_type=pl.DeviceIdType.MESH
        )

    pl.semaphore_signal(
        barrier, inc=1, device_id=sibling, device_id_type=pl.DeviceIdType.MESH
    )
    pl.semaphore_wait(barrier, devices)

    sib_copies = {}
    for i in turns:
        sib_copies[i] = send(
            gp.at[:, :, aligned(2 * plus(i) + 1 - c, width)],
            sibr.at[i],
            sib_ss.at[i],
            sib_rs.at[i],
            sibling,
        )

    r_copies = [
        send(
            rb.at[plus(i)],
            right.at[c, :, aligned(z, width)],
            r_ss.at[i],
            r_rs.at[i],
            peer(dp, plus(i)),
        )
        for i in range(1, nz)
    ]
    r_own = local(rb.at[z], right.at[c, :, aligned(z, width)], r_rs.at[0])

    step = 4
    rs_copies = []
    for i in turns:
        mine_copies[i].wait()
        sib_copies[i].wait_recv()
        if i:

            @pl.loop(0, blocks // step)
            def _(b):
                at = pl.ds(b * step, step)
                mine[i, at] = (mine[i, at].astype(f32) + sibr[i, at].astype(f32)).astype(bf16)

            rs_copies.append(
                send(mine.at[i], rsr.at[i], rs_ss.at[i], rs_rs.at[i], peer(dp, plus(i)))
            )
    for copy in rs_copies:
        copy.wait_recv()

    @pl.loop(0, blocks // step)
    def _(b):
        at = pl.ds(b * step, step)
        total = mine[0, at].astype(f32) + sibr[0, at].astype(f32)
        for i in range(1, nz):
            total = total + rsr[i, at].astype(f32)
        summed[at] = total.astype(bf16)

    summed[blocks] = jnp.zeros((rows, width), bf16)

    band_rows = aligned(dp, rows)
    band_cols = aligned(2 * z + c, width)

    def slot_rows(i):
        o, k = partner(i)
        s = o * nz + k
        stage[i] = summed[inv_ref[s]]
        return o, k

    @pl.loop(1, devices)
    def _(i):
        o, k = slot_rows(i)
        send(stage.at[i], grad.at[band_rows, band_cols], a_ss.at[0], a_rs.at[0], peer(o, k))

    slot_rows(0)
    local(stage.at[0], grad.at[band_rows, band_cols], a_rs.at[0])

    l_copies = [
        send(
            lb.at[plus(i)],
            left.at[aligned(2 * z + c, width)],
            l_ss.at[i],
            l_rs.at[i],
            peer(dp, plus(i)),
        )
        for i in range(1, nz)
    ]
    l_own = local(lb.at[z], left.at[aligned(2 * z + c, width)], l_rs.at[0])

    r_own.wait()
    for copy in r_copies:
        copy.wait_recv()
    r_sib = send(right.at[c], right.at[c], one_ss.at[0], one_rs.at[0], sibling)
    l_own.wait()
    for copy in l_copies:
        copy.wait_recv()
    l_sib = []
    for j in range(nz):
        band = left.at[aligned(2 * j + c, width)]
        l_sib.append(send(band, band, l_sib_ss.at[j], l_sib_rs.at[j], sibling))

    half = grad.at[:, pl.ds(0, nz * width)]
    pltpu.make_async_copy(half, half, a_rs.at[0]).wait()
    g_sib = []
    for j in range(nz):
        band = grad.at[:, aligned(2 * j + c, width)]
        g_sib.append(send(band, band, g_sib_ss.at[j], g_sib_rs.at[j], sibling))
    for copy in g_sib:
        copy.wait_recv()

    @pl.loop(0, CHUNKS)
    def _(r):
        at = aligned(r, size)
        rot[at] = dot(grad[at], right[c], ((1,), (0,))).astype(bf16)

    for copy in l_sib:
        copy.wait_recv()

    @pl.loop(0, CHUNKS)
    def _(r):
        at = aligned(r, size)
        eig[at] = dot(left[at], rot[...], ((1,), (0,))).astype(bf16)
        for i in range(1, nz):
            send(
                eig.at[at, aligned(plus(i), width)],
                ein.at[z, at],
                e_ss.at[i, r],
                e_rs.at[i, r],
                peer(dp, plus(i)),
            )
        local(eig.at[at, aligned(z, width)], ein.at[z, at], e_rs.at[0, r])

    @pl.loop(0, CHUNKS)
    def _(r):
        at = aligned(r, size)
        lhs = jnp.concatenate([grad[aligned(2 * j + c, width), :] for j in range(nz)], axis=0)
        out = dot(lhs, grad[at, :], ((1,), (1,))).astype(bf16)
        for j in range(nz):
            ggo[j, :, at] = out[j * width : (j + 1) * width]

    @pl.loop(0, CHUNKS)
    def _(r):
        at = aligned(r, size)
        lhs = jnp.concatenate([grad[:, aligned(2 * j + c, width)] for j in range(nz)], axis=1)
        out = dot(lhs, grad[:, at], ((0,), (0,))).astype(bf16)
        for j in range(nz):
            gto[j, :, at] = out[j * width : (j + 1) * width]

    load_first.wait()
    load_second.wait()

    @pl.loop(0, CHUNKS)
    def _(r):
        at = aligned(r, size)
        for i in list(range(1, nz)) + [0]:
            k = minus(i)
            piece = ein.at[k, at]
            pltpu.make_async_copy(piece, piece, e_rs.at[i, r]).wait()
            e = ein[k, at].astype(f32)
            new_first = first_beta * first[k, at] + (1.0 - first_beta) * e
            new_second = second_beta * second[k, at] + (1.0 - second_beta) * e * e
            nout[k, at] = (new_first / (jnp.sqrt(new_second) + epsilon)).astype(bf16)
            if i:
                send(
                    nout.at[k, at],
                    normed.at[at, aligned(z, width)],
                    n_ss.at[i, r],
                    n_rs.at[i, r],
                    peer(dp, k),
                )
            else:
                local(nout.at[k, at], normed.at[at, aligned(z, width)], n_rs.at[0, r])

    for i in range(nz):
        for r in range(CHUNKS):
            piece = normed.at[pl.ds(r * size, size), aligned(plus(i), width)]
            pltpu.make_async_copy(piece, piece, n_rs.at[i, r]).wait()

    def outer_send(out, into, ss, rs):
        copies = [
            send(out.at[plus(i)], into.at[z], ss.at[i], rs.at[i], peer(dp, plus(i)))
            for i in range(1, nz)
        ]
        return copies, local(out.at[z], into.at[z], rs.at[0])

    gg_copies, gg_own = outer_send(ggo, ggt_in, gg_ss, gg_rs)

    r_sib.wait_recv()

    @pl.loop(0, CHUNKS)
    def _(r):
        at = aligned(r, size)
        back[c, at] = dot(left[:, at], normed[...], ((0,), (0,))).astype(bf16)
        send(back.at[c, at], back.at[c, at], b_sib_ss.at[r], b_sib_rs.at[r], sibling)

    for r in range(CHUNKS):
        piece = back.at[1 - c, pl.ds(r * size, size)]
        pltpu.make_async_copy(piece, piece, b_sib_rs.at[r]).wait()

    per_chunk = n_dp // CHUNKS
    my_slot = dp * nz + z

    @pl.loop(0, CHUNKS)
    def _(r):
        rr = lax.rem(r + dp // per_chunk, CHUNKS)
        at = aligned(rr, size)
        total = None
        for p in range(2):
            rhs = jnp.concatenate(
                [right[p, aligned(2 * j + c, width), :] for j in range(nz)], axis=0
            )
            term = dot(back[p, at], rhs, ((1,), (1,)))
            total = term if total is None else total + term
        ucols[at] = total.astype(bf16)

        @pl.loop(0, per_chunk * nz)
        def _(q):
            dd = rr * per_chunk + lax.rem(dp + q // nz, per_chunk)
            j = lax.rem(z + q % nz, nz)
            src = ucols.at[aligned(dd, rows), aligned(j, width)]
            own = jnp.logical_and(dd == dp, j == z)

            @pl.when(own)
            def _():
                local(src, uin.at[my_slot], a_rs.at[1])

            @pl.when(jnp.logical_not(own))
            def _():
                send(src, uin.at[my_slot], a_ss.at[1], a_rs.at[1], peer(dd, j))

    gt_copies, gt_own = outer_send(gto, gtg_in, gt_ss, gt_rs)

    pltpu.make_async_copy(uin, uin, a_rs.at[1]).wait()

    @pl.loop(0, blocks)
    def _(b):
        upd[b] = uin[slot_ref[b]]

    for own, copies in ((gg_own, gg_copies), (gt_own, gt_copies)):
        own.wait()
        for copy in copies:
            copy.wait()
    for copies in (r_copies, l_copies, rs_copies, l_sib, g_sib, [r_sib]):
        for copy in copies:
            copy.wait_send()
    for i in turns:
        sib_copies[i].wait_send()
    sent = stage.at[pl.ds(0, devices - 1)]
    for n in range(2):
        pltpu.make_async_copy(sent, sent, a_ss.at[n]).wait()

    @pl.loop(0, CHUNKS)
    def _(r):
        at = aligned(r, size)
        for i in range(1, nz):
            piece = eig.at[at, aligned(plus(i), width)]
            pltpu.make_async_copy(piece, piece, e_ss.at[i, r]).wait()
            piece = nout.at[minus(i), at]
            pltpu.make_async_copy(piece, piece, n_ss.at[i, r]).wait()
        piece = back.at[c, at]
        pltpu.make_async_copy(piece, piece, b_sib_ss.at[r]).wait()


def run_step(slot_of_block, inverse, partial, left_basis, right_basis, first, second):
    blocks, rows, order = partial.shape
    nz, width = left_basis.shape[0], left_basis.shape[1]
    n_dp = lax.axis_size("dp")
    slots = n_dp * nz
    half = nz * width
    vmem = pl.BlockSpec(memory_space=pltpu.VMEM)
    smem = pl.BlockSpec(memory_space=pltpu.SMEM)
    anywhere = pl.BlockSpec(memory_space=pl.ANY)
    dma = pltpu.SemaphoreType.DMA
    scratch = [
        pltpu.VMEM((nz, blocks, rows, width), bf16),
        pltpu.VMEM((nz, blocks, rows, width), bf16),
        pltpu.VMEM((nz, blocks, rows, width), bf16),
        pltpu.VMEM((blocks + 1, rows, width), bf16),
        pltpu.VMEM((slots, rows, width), bf16),
        pltpu.VMEM((order, order), bf16),
        pltpu.VMEM((order, order), bf16),
        pltpu.VMEM((2, order, half), bf16),
        pltpu.VMEM((order, half), bf16),
        pltpu.VMEM((order, half), bf16),
        pltpu.VMEM((nz, order, width), f32),
        pltpu.VMEM((nz, order, width), f32),
        pltpu.VMEM((nz, order, width), bf16),
        pltpu.VMEM((order, half), bf16),
        pltpu.VMEM((2, order, half), bf16),
        pltpu.VMEM((nz, width, order), bf16),
        pltpu.VMEM((nz, width, order), bf16),
        pltpu.VMEM((order, half), bf16),
        pltpu.VMEM((slots, rows, width), bf16),
        dma((2,)),
        dma((nz,)),
        dma((nz,)),
        dma((nz,)),
        dma((nz,)),
        dma((nz,)),
        dma((2,)),
        dma((2,)),
        dma((nz,)),
        dma((nz,)),
        dma((nz,)),
        dma((nz,)),
        dma((nz,)),
        dma((nz,)),
        dma((nz,)),
        dma((nz,)),
        dma((nz, CHUNKS)),
        dma((nz, CHUNKS)),
        dma((nz, CHUNKS)),
        dma((nz, CHUNKS)),
        dma((nz,)),
        dma((nz,)),
        dma((nz,)),
        dma((nz,)),
        dma((CHUNKS,)),
        dma((CHUNKS,)),
        dma((1,)),
        dma((1,)),
    ]
    return pl.pallas_call(
        functools.partial(step_kernel, n_dp, nz),
        out_shape=(
            jax.ShapeDtypeStruct((blocks, rows, width), bf16),
            jax.ShapeDtypeStruct((nz, order, width), bf16),
            jax.ShapeDtypeStruct((nz, width, order), bf16),
            jax.ShapeDtypeStruct((nz, width, order), bf16),
        ),
        in_specs=[smem, smem] + [anywhere] * 5,
        out_specs=(vmem, vmem, vmem, vmem),
        scratch_shapes=scratch,
        compiler_params=pltpu.CompilerParams(
            collective_id=0, has_side_effects=True, vmem_limit_bytes=56 * 2**20
        ),
        cost_estimate=pl.CostEstimate(
            flops=12 * order * order * half, bytes_accessed=16 * 2**20, transcendentals=0
        ),
        name="soap_step",
    )(slot_of_block, inverse, partial, left_basis, right_basis, first, second)


def per_device(
    grad_partial,
    slot_of_block,
    left_factor,
    right_factor,
    left_basis,
    right_basis,
    first_moment,
    second_moment,
):
    blocks = grad_partial.shape[1]
    slots = lax.axis_size("dp") * left_factor.shape[0]
    slot_ids = jnp.arange(slots, dtype=jnp.int32)
    taken = slot_ids[:, None] == slot_of_block[None, :]
    offsets = jnp.arange(blocks, dtype=jnp.int32) - blocks
    inverse = blocks + jnp.sum(jnp.where(taken, offsets[None, :], 0), axis=1, dtype=jnp.int32)
    update, eigen, outer_left, outer_right = run_step(
        slot_of_block,
        inverse,
        grad_partial[0],
        left_basis,
        right_basis,
        first_moment,
        second_moment,
    )
    eigen = eigen.astype(f32)
    new_left = second_beta * left_factor + (1.0 - second_beta) * outer_left.astype(f32)
    new_right = second_beta * right_factor + (1.0 - second_beta) * outer_right.astype(f32)
    new_first = first_beta * first_moment + (1.0 - first_beta) * eigen
    new_second = second_beta * second_moment + (1.0 - second_beta) * eigen * eigen
    return (update, new_left, new_right, new_first, new_second)


def solution(mesh):
    in_specs = (
        P("tensor", None, "dp", None),
        P(),
        P("dp", "tensor", None),
        P("dp", "tensor", None),
        P("dp", "tensor", None),
        P("dp", None, "tensor"),
        P("dp", None, "tensor"),
        P("dp", None, "tensor"),
    )
    out_specs = (
        P(None, "dp", "tensor"),
        P("dp", "tensor", None),
        P("dp", "tensor", None),
        P("dp", None, "tensor"),
        P("dp", None, "tensor"),
    )
    return jax.shard_map(
        per_device, mesh=mesh, in_specs=in_specs, out_specs=out_specs, check_vma=False
    )
```

time: 307 us -> 153 us (0.50)
  waiting for transfers between devices: 166 us -> 0 us
  Pallas kernels: 0 us -> 142 us
  local copies, waits for them, and re-layouts: 57 us -> 0.82 us
  matrix products: 40.7 us -> 0 us
  blocking collectives: 19.5 us -> 0 us
  between operations: 13.9 us -> 0.7 us
  other arithmetic: 0 us -> 8.66 us
  starting transfers between devices: 6.88 us -> 0 us
    pallas_call x0 -> x1, Pallas kernels: none -> 142 us  [run_step(): pl.pallas_call(functools.partial(step_kernel, n_dp, nz), out_shape=(jax.S...]
    unnamed x6 -> x0, waiting for transfers between devices: 86.3 us -> none
    all_gather x2 -> x0, waiting for transfers between devices: 79.5 us -> none  [the longest x1 56.5 us: per_device(): lax.all_gather(grad_slots, 'tensor', axis=2, tiled=True)]
    unnamed x22 -> x13, local copies, waits for them, and re-layouts: 51.3 us -> 0.82 us
    dot_general x6 -> x0, matrix products: 40.7 us -> none  [the longest x1 15.1 us: per_device(): jnp.einsum('jak,jkr->jar', full_left, rotated, preferred_element_type=jnp...]
    all_to_all x1 -> x0, blocking collectives: 19.5 us -> none  [per_device(): lax.all_to_all(outgoing, 'dp', split_axis=0, concat_axis=0, tiled=True)]
    add x0 -> x3, other arithmetic: none -> 7.91 us  [the longest x1 4.79 us: per_device(): second_beta * right_factor + (1.0 - second_beta) * outer_right.astype(f32)]
    all_to_all x1 -> x0, starting transfers between devices: 6.54 us -> none  [per_device(): lax.all_to_all(update_cols, 'dp', split_axis=2, concat_axis=1, tiled=True)]
  transfers between devices with their start and end apart: 5 -> 0, of which waited for: 4 -> 0; matrix products, arithmetic and copies ran while one was open for 10% -> 0% of each run, Pallas kernels for 0% -> 0%
where the time goes in v2:
time: 153 us
  Pallas kernels  142 us (93%)
  other arithmetic  8.66 us (6%)
    pallas_call x1, Pallas kernels, run_step(): pl.pallas_call(functools.partial(step_kernel, n_dp, nz), out_shape=(jax.S...  142 us
    add x1, other arithmetic, per_device(): second_beta * right_factor + (1.0 - second_beta) * outer_right.astype(f32)  4.79 us

profile of v2, /device:TPU:1, one launch (start us, length us, event | category | flops | bytes accessed | tf_op | source)
XLA Modules:
  0.0 152.6 jit_solution(10250560235926696175)
XLA Ops:
  0.6 0.7 select_reduce_fusion
  1.4 0.5 broadcast_add_fusion.inv_ref
  1.9 0.0 copy-start
  1.9 0.0 copy-start.1
  1.9 142.4 %soap_step.1 = (bf16[32,64,128]{2,1,0:T(8,128)(2,1)}, bf16[4,1024,128]{2,1,0:T(8,128)(2,1)}, bf16[4,128,1024]{2,1,0:T(8,128)(2,1)}, bf16[4,128,1024]{2,1,0:T(8,128)(2,1)}) custom-call(s32[32]{0:T(128)} %slot_ref.1, s32[64]{0:T(128)} %broadcast_add_fusion.inv_ref, bf16[32,64,1024]{2,1,0:T(8,128)(2,1)} %bitcast.1, bf16[4,128,1024]{2,1,0:T(8,128)(2,1)} %lb.1, ...), custom_call_target="tpu_custom_call" | custom-call | flops 6442450944 | bytes 16777216 | tf_op jit(solution)/shard_map/soap_step/pallas_call | solution.py:461
  144.3 0.0 copy-done
  144.3 0.0 copy-done.1
  144.3 0.0 copy-start.2
  144.3 0.0 copy-start.3
  144.3 0.0 copy-start.4
  144.4 4.8 %multiply_add_fusion = (f32[4,128,1024]{2,1,0:T(8,128)}, f32[4,128,1024]{2,1,0:T(8,128)}) fusion(bf16[4,128,1024]{2,1,0:T(8,128)(2,1)} %get-tuple-element.11, f32[4,128,1024]{2,1,0:T(8,128)S(1)} %copy-done, bf16[4,128,1024]{2,1,0:T(8,128)(2,1)} %get-tuple-element.10, f32[4,128,1024]{2,1,0:T(8,128)S(1)} %copy-done.1), kind=kLoop, calls=%fused_computation.4 | loop fusion | flops 4194304 | bytes 10485760 | tf_op jit(solution)/shard_map/add | solution.py:509
  149.1 0.0 copy-done.2
  149.1 0.0 copy-done.3
  149.1 0.0 copy-done.4
  149.2 0.0 copy-start.5
  149.2 2.6 %fusion.1 = (f32[4,1024,128]{2,1,0:T(8,128)}, f32[4,1024,128]{2,1,0:T(8,128)}) fusion(bf16[4,1024,128]{2,1,0:T(8,128)(2,1)S(1)} %copy-done.4, f32[4,1024,128]{2,1,0:T(8,128)S(1)} %copy-done.3, f32[4,1024,128]{2,1,0:T(8,128)S(1)} %copy-done.2), kind=kLoop, calls=%fused_computation.3 | loop fusion | flops 4194304 | bytes 9437184 | tf_op jit(solution)/shard_map/add | solution.py:511
  151.8 0.0 copy-done.5
  151.8 0.8 copy.14
  (1 shorter events, 0.0 us)
Async XLA Ops:
  1.9 142.4 %copy-start = (f32[4,128,1024]{2,1,0:T(8,128)S(1)}, f32[4,128,1024]{2,1,0:T(8,128)}, u32[]{:S(2)}) copy-start(f32[4,128,1024]{2,1,0:T(8,128)} %param.11) | copy-start | bytes 6291460
  1.9 142.4 %copy-start.1 = (f32[4,128,1024]{2,1,0:T(8,128)S(1)}, f32[4,128,1024]{2,1,0:T(8,128)}, u32[]{:S(2)}) copy-start(f32[4,128,1024]{2,1,0:T(8,128)} %param.10) | copy-start | bytes 6291460
  144.3 4.8 %copy-start.2 = (f32[4,1024,128]{2,1,0:T(8,128)S(1)}, f32[4,1024,128]{2,1,0:T(8,128)}, u32[]{:S(2)}) copy-start(f32[4,1024,128]{2,1,0:T(8,128)} %first_hbm.1) | copy-start | bytes 6291460
  144.3 4.8 %copy-start.3 = (f32[4,1024,128]{2,1,0:T(8,128)S(1)}, f32[4,1024,128]{2,1,0:T(8,128)}, u32[]{:S(2)}) copy-start(f32[4,1024,128]{2,1,0:T(8,128)} %second_hbm.1) | copy-start | bytes 6291460
  144.3 4.8 %copy-start.4 = (bf16[4,1024,128]{2,1,0:T(8,128)(2,1)S(1)}, bf16[4,1024,128]{2,1,0:T(8,128)(2,1)}, u32[]{:S(2)}) copy-start(bf16[4,1024,128]{2,1,0:T(8,128)(2,1)} %get-tuple-element.12) | copy-start | bytes 3145732
  149.2 2.6 %copy-start.5 = (bf16[32,64,128]{2,1,0:T(8,128)(2,1)S(1)}, bf16[32,64,128]{2,1,0:T(8,128)(2,1)}, u32[]{:S(2)}) copy-start(bf16[32,64,128]{2,1,0:T(8,128)(2,1)} %get-tuple-element.22) | copy-start | bytes 1572868

commit v3 on v2

v3 whole, which is shorter than its diff:
```python
import functools
import jax
import jax.numpy as jnp
from jax import lax
from jax.experimental import pallas as pl
from jax.experimental.pallas import tpu as pltpu
from jax.sharding import PartitionSpec as P

first_beta = 0.9
second_beta = 0.95
epsilon = 1e-08
f32 = jnp.float32
bf16 = jnp.bfloat16
CHUNKS = 4


def aligned(index, size):
    return pl.ds(pl.multiple_of(index * size, size), size)


def dot(a, b, dims):
    return lax.dot_general(a, b, (dims, ((), ())), preferred_element_type=f32)


def step_kernel(
    n_dp,
    nz,
    slot_ref,
    gp,
    lb,
    rb,
    left_hbm,
    right_hbm,
    first_hbm,
    second_hbm,
    upd,
    new_left,
    new_right,
    first,
    second,
    inv_ref,
    ein,
    ggt_in,
    gtg_in,
    mine,
    sibr,
    rsr,
    summed,
    stage,
    grad,
    left,
    right,
    rot,
    eig,
    nout,
    normed,
    back,
    ggo,
    gto,
    ucols,
    uin,
    load_sem,
    mine_sem,
    sib_ss,
    sib_rs,
    rs_ss,
    rs_rs,
    a_ss,
    a_rs,
    r_ss,
    r_rs,
    l_ss,
    l_rs,
    gg_ss,
    gg_rs,
    gt_ss,
    gt_rs,
    e_ss,
    e_rs,
    n_ss,
    n_rs,
    g_sib_ss,
    g_sib_rs,
    l_sib_ss,
    l_sib_rs,
    b_sib_ss,
    b_sib_rs,
    one_ss,
    one_rs,
    known,
):
    blocks, rows, order = gp.shape
    width = lb.shape[1]
    size = order // CHUNKS
    dp = lax.axis_index("dp")
    t = lax.axis_index("tensor")
    z = t // 2
    c = t % 2
    sibling = (dp, 2 * z + 1 - c)
    devices = n_dp * nz
    ny = n_dp // CHUNKS
    x = dp // ny
    y = dp % ny

    def peer(o, k):
        return (o, 2 * k + c)

    def send(src, dst, ss, rs, dev):
        copy = pltpu.make_async_remote_copy(
            src_ref=src,
            dst_ref=dst,
            send_sem=ss,
            recv_sem=rs,
            device_id=dev,
            device_id_type=pl.DeviceIdType.MESH,
        )
        copy.start()
        return copy

    def local(src, dst, sem):
        copy = pltpu.make_async_copy(src, dst, sem)
        copy.start()
        return copy

    def plus(i):
        return lax.rem(z + i, nz)

    def minus(i):
        return lax.rem(z + nz - i, nz)

    def partner(i):
        xx = lax.rem(x + i // (ny * nz), CHUNKS)
        yy = lax.rem(y + (i // nz) % ny, ny)
        return xx * ny + yy, lax.rem(z + i % nz, nz)

    def signal(sem, dev):
        pl.semaphore_signal(sem, inc=1, device_id=dev, device_id_type=pl.DeviceIdType.MESH)

    turns = (2, 1, nz - 1, 0)
    mine_copies = {}
    for i in turns:
        mine_copies[i] = local(
            gp.at[:, :, aligned(2 * plus(i) + c, width)], mine.at[i], mine_sem.at[i]
        )

    barrier = pltpu.get_barrier_semaphore()
    line_z = [peer(dp, plus(i)) for i in range(1, nz)]
    line_x = [peer(lax.rem(x + i, CHUNKS) * ny + y, z) for i in range(1, CHUNKS)]
    line_y = [peer(x * ny + lax.rem(y + i, ny), z) for i in range(1, ny)]
    greeted = [sibling] + line_z + line_x + line_y
    for dev in greeted:
        signal(barrier, dev)

    @pl.loop(0, devices)
    def _(i):
        found = jnp.int32(blocks)
        for b in range(blocks):
            found = jnp.where(slot_ref[b] == i, jnp.int32(b), found)
        inv_ref[i] = found

    pl.semaphore_wait(barrier, len(greeted))
    for dev in line_x:
        signal(known.at[0], dev)

    sib_copies = {}
    for i in turns:
        sib_copies[i] = send(
            gp.at[:, :, aligned(2 * plus(i) + 1 - c, width)],
            sibr.at[i],
            sib_ss.at[i],
            sib_rs.at[i],
            sibling,
        )

    r_copies = [
        send(
            rb.at[plus(i)],
            right.at[c, :, aligned(z, width)],
            r_ss.at[i],
            r_rs.at[i],
            peer(dp, plus(i)),
        )
        for i in range(1, nz)
    ]
    r_own = local(rb.at[z], right.at[c, :, aligned(z, width)], r_rs.at[0])

    step = 4
    part = blocks // 2
    low, high = pl.ds(0, part), pl.ds(part, part)

    def add(i, start, other):
        @pl.loop(0, part // step)
        def _(b):
            at = pl.ds(start + b * step, step)
            mine[i, at] = (mine[i, at].astype(f32) + other[at].astype(f32)).astype(bf16)

    def pass_on(i, at, into, n, hop):
        return send(mine.at[i, at], into, rs_ss.at[n], rs_rs.at[n], peer(dp, plus(hop)))

    def two_cores(i):
        mine_copies[i].wait()
        sib_copies[i].wait_recv()
        add(i, 0, sibr.at[i])
        add(i, part, sibr.at[i])

    last = nz - 1
    two_cores(2)
    pl.semaphore_wait(known.at[0], len(line_x))
    for dev in line_z:
        signal(known.at[1], dev)
    up = pass_on(2, low, rsr.at[0, low], 0, 1)
    down = pass_on(2, high, rsr.at[0, high], 1, last)
    two_cores(1)
    up_direct = pass_on(1, high, rsr.at[1, high], 2, 1)
    two_cores(last)
    down_direct = pass_on(last, low, rsr.at[2, low], 3, last)
    up.wait_recv()
    add(1, 0, rsr.at[0])
    up_sum = pass_on(1, low, rsr.at[1, low], 4, 1)
    down.wait_recv()
    add(last, part, rsr.at[0])
    down_sum = pass_on(last, high, rsr.at[2, high], 5, last)
    rs_copies = [up, down, up_direct, down_direct, up_sum, down_sum]
    mine_copies[0].wait()
    sib_copies[0].wait_recv()

    load_first = local(first_hbm, first, load_sem.at[0])
    load_second = local(second_hbm, second, load_sem.at[1])
    load_left = local(left_hbm, new_left, load_sem.at[2])
    load_right = local(right_hbm, new_right, load_sem.at[3])

    l_copies = [
        send(
            lb.at[plus(i)],
            left.at[aligned(2 * z + c, width)],
            l_ss.at[i],
            l_rs.at[i],
            peer(dp, plus(i)),
        )
        for i in range(1, nz)
    ]
    l_own = local(lb.at[z], left.at[aligned(2 * z + c, width)], l_rs.at[0])

    for copy in rs_copies[2:]:
        copy.wait_recv()

    @pl.loop(0, blocks // step)
    def _(b):
        at = pl.ds(b * step, step)
        total = mine[0, at].astype(f32) + sibr[0, at].astype(f32)
        total = total + rsr[1, at].astype(f32) + rsr[2, at].astype(f32)
        summed[at] = total.astype(bf16)

    summed[blocks] = jnp.zeros((rows, width), bf16)

    band = grad.at[c, aligned(dp, rows), aligned(z, width)]
    pl.semaphore_wait(known.at[1], len(line_z))

    def slot_rows(i):
        o, k = partner(i)
        stage[i] = summed[inv_ref[o * nz + k]]
        return o, k

    slot_rows(0)
    local(stage.at[0], band, a_rs.at[0])

    @pl.loop(1, devices)
    def _(i):
        o, k = slot_rows(i)
        send(stage.at[i], band, a_ss.at[0], a_rs.at[i // (ny * nz)], peer(o, k))

    r_own.wait()
    for copy in r_copies:
        copy.wait_recv()
    r_sib = send(right.at[c], right.at[c], one_ss.at[0], one_rs.at[0], sibling)
    l_own.wait()
    for copy in l_copies:
        copy.wait_recv()
    l_sib = []
    for j in range(nz):
        band = left.at[aligned(2 * j + c, width)]
        l_sib.append(send(band, band, l_sib_ss.at[j], l_sib_rs.at[j], sibling))

    def rotate(r):
        at = aligned(lax.rem(x + CHUNKS - r, CHUNKS), size)
        g_sib[r].wait_recv()
        total = None
        for p in range(2):
            rhs = jnp.concatenate(
                [right[c, pl.ds((2 * j + p) * width, width), :] for j in range(nz)], axis=0
            )
            term = dot(grad[p, at], rhs, ((1,), (0,)))
            total = term if total is None else total + term
        rot[at] = total.astype(bf16)

    g_sib = []
    for r in range(CHUNKS):
        piece = grad.at[c, aligned(lax.rem(x + CHUNKS - r, CHUNKS), size)]
        pltpu.make_async_copy(piece, piece, a_rs.at[r]).wait()
        g_sib.append(send(piece, piece, g_sib_ss.at[r], g_sib_rs.at[r], sibling))
        if r:
            rotate(r - 1)
    rotate(CHUNKS - 1)

    for copy in l_sib:
        copy.wait_recv()

    @pl.loop(0, CHUNKS)
    def _(r):
        at = aligned(r, size)
        eig[at] = dot(left[at], rot[...], ((1,), (0,))).astype(bf16)
        for i in range(1, nz):
            send(
                eig.at[at, aligned(plus(i), width)],
                ein.at[z, at],
                e_ss.at[i, r],
                e_rs.at[i, r],
                peer(dp, plus(i)),
            )
        local(eig.at[at, aligned(z, width)], ein.at[z, at], e_rs.at[0, r])

    @pl.loop(0, CHUNKS)
    def _(r):
        at = aligned(r, size)
        out = None
        for p in range(2):
            lhs = jnp.concatenate(
                [grad[p, aligned(2 * j + c, width), :] for j in range(nz)], axis=0
            )
            term = dot(lhs, grad[p, at], ((1,), (1,)))
            out = term if out is None else out + term
        out = out.astype(bf16)
        for j in range(nz):
            ggo[j, :, at] = out[j * width : (j + 1) * width]

    pair = nz // 2

    @pl.loop(0, 4)
    def _(r):
        p, h = r // 2, r % 2
        rhs = grad[p, :, aligned(h, pair * width)]
        out = dot(grad[c], rhs, ((0,), (0,))).astype(bf16)
        for j in range(nz):
            for n in range(pair):
                at = aligned(2 * (pair * h + n) + p, width)
                gto[j, :, at] = out[j * width : (j + 1) * width, n * width : (n + 1) * width]

    load_first.wait()
    load_second.wait()

    @pl.loop(0, CHUNKS)
    def _(r):
        at = aligned(r, size)
        for i in list(range(1, nz)) + [0]:
            k = minus(i)
            piece = ein.at[k, at]
            pltpu.make_async_copy(piece, piece, e_rs.at[i, r]).wait()
            e = ein[k, at].astype(f32)
            new_first = first_beta * first[k, at] + (1.0 - first_beta) * e
            new_second = second_beta * second[k, at] + (1.0 - second_beta) * e * e
            first[k, at] = new_first
            second[k, at] = new_second
            nout[k, at] = (new_first / (jnp.sqrt(new_second) + epsilon)).astype(bf16)
            if i:
                send(
                    nout.at[k, at],
                    normed.at[at, aligned(z, width)],
                    n_ss.at[i, r],
                    n_rs.at[i, r],
                    peer(dp, k),
                )
            else:
                local(nout.at[k, at], normed.at[at, aligned(z, width)], n_rs.at[0, r])

    def outer_send(out, into, ss, rs):
        copies = [
            send(out.at[plus(i)], into.at[z], ss.at[i], rs.at[i], peer(dp, plus(i)))
            for i in range(1, nz)
        ]
        return copies, local(out.at[z], into.at[z], rs.at[0])

    gg_copies, gg_own = outer_send(ggo, ggt_in, gg_ss, gg_rs)

    for i in range(nz):
        for r in range(CHUNKS):
            piece = normed.at[pl.ds(r * size, size), aligned(plus(i), width)]
            pltpu.make_async_copy(piece, piece, n_rs.at[i, r]).wait()

    r_sib.wait_recv()

    @pl.loop(0, CHUNKS)
    def _(r):
        at = aligned(r, size)
        back[c, at] = dot(left[:, at], normed[...], ((0,), (0,))).astype(bf16)
        send(back.at[c, at], back.at[c, at], b_sib_ss.at[r], b_sib_rs.at[r], sibling)

    for r in range(CHUNKS):
        piece = back.at[1 - c, pl.ds(r * size, size)]
        pltpu.make_async_copy(piece, piece, b_sib_rs.at[r]).wait()

    per_chunk = n_dp // CHUNKS
    my_slot = dp * nz + z

    @pl.loop(0, CHUNKS)
    def _(r):
        rr = lax.rem(r + dp // per_chunk, CHUNKS)
        at = aligned(rr, size)
        total = None
        for p in range(2):
            rhs = jnp.concatenate(
                [right[p, aligned(2 * j + c, width), :] for j in range(nz)], axis=0
            )
            term = dot(back[p, at], rhs, ((1,), (1,)))
            total = term if total is None else total + term
        ucols[at] = total.astype(bf16)

        @pl.loop(0, per_chunk * nz)
        def _(q):
            dd = rr * per_chunk + lax.rem(dp + q // nz, per_chunk)
            j = lax.rem(z + q % nz, nz)
            src = ucols.at[aligned(dd, rows), aligned(j, width)]
            own = jnp.logical_and(dd == dp, j == z)

            @pl.when(own)
            def _():
                local(src, uin.at[my_slot], a_rs.at[CHUNKS])

            @pl.when(jnp.logical_not(own))
            def _():
                send(src, uin.at[my_slot], a_ss.at[1], a_rs.at[CHUNKS], peer(dd, j))

    gt_copies, gt_own = outer_send(gto, gtg_in, gt_ss, gt_rs)

    def factors(load, into, outer, own, copies):
        load.wait()
        for i in range(nz):
            k = minus(i)
            (copies[i - 1].wait_recv if i else own.wait)()

            @pl.loop(0, width // 32)
            def _(b):
                at = pl.ds(b * 32, 32)
                into[k, at] = second_beta * into[k, at] + (1.0 - second_beta) * outer[
                    k, at
                ].astype(f32)

    factors(load_left, new_left, ggt_in, gg_own, gg_copies)
    pltpu.make_async_copy(uin, uin, a_rs.at[CHUNKS]).wait()

    @pl.loop(0, blocks)
    def _(b):
        upd[b] = uin[slot_ref[b]]

    factors(load_right, new_right, gtg_in, gt_own, gt_copies)

    for copies in (r_copies, l_copies, rs_copies, l_sib, g_sib, [r_sib], gg_copies, gt_copies):
        for copy in copies:
            copy.wait_send()
    for i in turns:
        sib_copies[i].wait_send()
    sent = stage.at[pl.ds(0, devices - 1)]
    for n in range(2):
        pltpu.make_async_copy(sent, sent, a_ss.at[n]).wait()

    @pl.loop(0, CHUNKS)
    def _(r):
        at = aligned(r, size)
        for i in range(1, nz):
            piece = eig.at[at, aligned(plus(i), width)]
            pltpu.make_async_copy(piece, piece, e_ss.at[i, r]).wait()
            piece = nout.at[minus(i), at]
            pltpu.make_async_copy(piece, piece, n_ss.at[i, r]).wait()
        piece = back.at[c, at]
        pltpu.make_async_copy(piece, piece, b_sib_ss.at[r]).wait()


def run_step(
    slot_of_block, partial, left_basis, right_basis, left_factor, right_factor, first, second
):
    blocks, rows, order = partial.shape
    nz, width = left_basis.shape[0], left_basis.shape[1]
    n_dp = lax.axis_size("dp")
    slots = n_dp * nz
    half = nz * width
    large = (partial, left_basis, right_basis, left_factor, right_factor, first, second)
    large = [pltpu.with_memory_space_constraint(array, pltpu.HBM) for array in large]
    vmem = pl.BlockSpec(memory_space=pltpu.VMEM)
    smem = pl.BlockSpec(memory_space=pltpu.SMEM)
    hbm = pl.BlockSpec(memory_space=pltpu.HBM)
    dma = pltpu.SemaphoreType.DMA
    scratch = [
        pltpu.SMEM((slots,), jnp.int32),
        pltpu.VMEM((nz, order, width), bf16),
        pltpu.VMEM((nz, width, order), bf16),
        pltpu.VMEM((nz, width, order), bf16),
        pltpu.VMEM((nz, blocks, rows, width), bf16),
        pltpu.VMEM((nz, blocks, rows, width), bf16),
        pltpu.VMEM((3, blocks, rows, width), bf16),
        pltpu.VMEM((blocks + 1, rows, width), bf16),
        pltpu.VMEM((slots, rows, width), bf16),
        pltpu.VMEM((2, order, half), bf16),
        pltpu.VMEM((order, order), bf16),
        pltpu.VMEM((2, order, half), bf16),
        pltpu.VMEM((order, half), bf16),
        pltpu.VMEM((order, half), bf16),
        pltpu.VMEM((nz, order, width), bf16),
        pltpu.VMEM((order, half), bf16),
        pltpu.VMEM((2, order, half), bf16),
        pltpu.VMEM((nz, width, order), bf16),
        pltpu.VMEM((nz, width, order), bf16),
        pltpu.VMEM((order, half), bf16),
        pltpu.VMEM((slots, rows, width), bf16),
        dma((4,)),
        dma((nz,)),
        dma((nz,)),
        dma((nz,)),
        dma((6,)),
        dma((6,)),
        dma((2,)),
        dma((CHUNKS + 1,)),
        dma((nz,)),
        dma((nz,)),
        dma((nz,)),
        dma((nz,)),
        dma((nz,)),
        dma((nz,)),
        dma((nz,)),
        dma((nz,)),
        dma((nz, CHUNKS)),
        dma((nz, CHUNKS)),
        dma((nz, CHUNKS)),
        dma((nz, CHUNKS)),
        dma((CHUNKS,)),
        dma((CHUNKS,)),
        dma((nz,)),
        dma((nz,)),
        dma((CHUNKS,)),
        dma((CHUNKS,)),
        dma((1,)),
        dma((1,)),
        pltpu.SemaphoreType.REGULAR((2,)),
    ]
    return pl.pallas_call(
        functools.partial(step_kernel, n_dp, nz),
        out_shape=(
            jax.ShapeDtypeStruct((blocks, rows, width), bf16),
            jax.ShapeDtypeStruct((nz, width, order), f32),
            jax.ShapeDtypeStruct((nz, width, order), f32),
            jax.ShapeDtypeStruct((nz, order, width), f32),
            jax.ShapeDtypeStruct((nz, order, width), f32),
        ),
        in_specs=[smem] + [hbm] * 7,
        out_specs=(vmem,) * 5,
        scratch_shapes=scratch,
        compiler_params=pltpu.CompilerParams(
            collective_id=0, has_side_effects=True, vmem_limit_bytes=40 * 2**20
        ),
        cost_estimate=pl.CostEstimate(
            flops=12 * order * order * half, bytes_accessed=16 * 2**20, transcendentals=0
        ),
        name="soap_step",
    )(slot_of_block, *large)


def per_device(
    grad_partial,
    slot_of_block,
    left_factor,
    right_factor,
    left_basis,
    right_basis,
    first_moment,
    second_moment,
):
    return run_step(
        slot_of_block,
        grad_partial[0],
        left_basis,
        right_basis,
        left_factor,
        right_factor,
        first_moment,
        second_moment,
    )


def solution(mesh):
    in_specs = (
        P("tensor", None, "dp", None),
        P(),
        P("dp", "tensor", None),
        P("dp", "tensor", None),
        P("dp", "tensor", None),
        P("dp", None, "tensor"),
        P("dp", None, "tensor"),
        P("dp", None, "tensor"),
    )
    out_specs = (
        P(None, "dp", "tensor"),
        P("dp", "tensor", None),
        P("dp", "tensor", None),
        P("dp", None, "tensor"),
        P("dp", None, "tensor"),
    )
    return jax.shard_map(
        per_device, mesh=mesh, in_specs=in_specs, out_specs=out_specs, check_vma=False
    )
```

time: 153 us -> 135 us (0.88)
  Pallas kernels: 142 us -> 127 us
  other arithmetic: 8.66 us -> 0 us
  local copies, waits for them, and re-layouts: 0.82 us -> 6.72 us
    pallas_call x1, Pallas kernels: 142 us -> 127 us  [run_step(): pl.pallas_call(functools.partial(step_kernel, n_dp, nz), out_shape=(jax.S...]
    add x3 -> x0, other arithmetic: 7.91 us -> none  [the longest x1 4.79 us: per_device(): second_beta * right_factor + (1.0 - second_beta) * outer_right.astype(f32)]
    unnamed x13 -> x7, local copies, waits for them, and re-layouts: 0.82 us -> 6.72 us
where the time goes in v3:
time: 135 us; the launch traced here: 134 us
  Pallas kernels  127 us (94%)
  local copies, waits for them, and re-layouts  6.72 us (5%)
    pallas_call x1, Pallas kernels, run_step(): pl.pallas_call(functools.partial(step_kernel, n_dp, nz), out_shape=(jax.S...  127 us
    unnamed x7, local copies, waits for them, and re-layouts  6.72 us

profile of v3, /device:TPU:1, one launch (start us, length us, event | category | flops | bytes accessed | tf_op | source)
XLA Modules:
  0.0 134.4 jit_solution(9936272830115069392)
XLA Ops:
  0.6 0.0 copy-start
  0.6 0.6 copy-done
  1.3 127.0 %soap_step.1 = (bf16[32,64,128]{2,1,0:T(8,128)(2,1)S(1)}, f32[4,128,1024]{2,1,0:T(8,128)S(1)}, f32[4,128,1024]{2,1,0:T(8,128)S(1)}, f32[4,1024,128]{2,1,0:T(8,128)S(1)}, f32[4,1024,128]{2,1,0:T(8,128)S(1)}) custom-call(s32[32]{0:T(128)S(1)} %copy-done, bf16[32,64,1024]{2,1,0:T(8,128)(2,1)} %bitcast.1, bf16[4,128,1024]{2,1,0:T(8,128)(2,1)} %lb.1, ...), custom_call_target="tpu_custom_call" | custom-call | flops 6442450944 | bytes 16777216 | tf_op jit(solution)/shard_map/soap_step/pallas_call | solution.py:543
  128.3 0.8 copy.18
  129.1 1.3 copy.19
  130.4 1.3 copy.20
  131.8 1.3 copy.21
  133.1 1.3 copy.22
Async XLA Ops:
  0.6 0.7 copy-start

commit v4 on v3

--- a/solution.py
+++ b/solution.py
@@ -25,7 +25,7 @@
 def step_kernel(
     n_dp,
     nz,
-    slot_ref,
+    slot_hbm,
     gp,
     lb,
     rb,
@@ -38,6 +38,7 @@
     new_right,
     first,
     second,
+    slot_ref,
     inv_ref,
     ein,
     ggt_in,
@@ -92,6 +93,8 @@
     blocks, rows, order = gp.shape
     width = lb.shape[1]
     size = order // CHUNKS
+    band_size = width // CHUNKS
+    band_half = width // 2
     dp = lax.axis_index("dp")
     t = lax.axis_index("tensor")
     z = t // 2
@@ -136,6 +139,7 @@
     def signal(sem, dev):
         pl.semaphore_signal(sem, inc=1, device_id=dev, device_id_type=pl.DeviceIdType.MESH)
 
+    slot_copy = local(slot_hbm, slot_ref, load_sem.at[4])
     turns = (2, 1, nz - 1, 0)
     mine_copies = {}
     for i in turns:
@@ -151,6 +155,7 @@
     for dev in greeted:
         signal(barrier, dev)
 
+    slot_copy.wait()
     @pl.loop(0, devices)
     def _(i):
         found = jnp.int32(blocks)
@@ -229,17 +234,25 @@
     load_left = local(left_hbm, new_left, load_sem.at[2])
     load_right = local(right_hbm, new_right, load_sem.at[3])
 
-    l_copies = [
-        send(
-            lb.at[plus(i)],
-            left.at[aligned(2 * z + c, width)],
-            l_ss.at[i],
-            l_rs.at[i],
-            peer(dp, plus(i)),
-        )
-        for i in range(1, nz)
-    ]
-    l_own = local(lb.at[z], left.at[aligned(2 * z + c, width)], l_rs.at[0])
+    def left_part(h):
+        at = pl.ds(h * band_half, band_half)
+        band = left.at[z, c, at]
+        copies = [
+            send(
+                lb.at[plus(i), at], band, l_ss.at[h, i], l_rs.at[h, i], peer(dp, plus(i))
+            )
+            for i in range(1, nz)
+        ]
+        return copies, local(lb.at[z, at], band, l_rs.at[h, 0])
+
+    def left_sibling(h, copies, own):
+        own.wait()
+        for copy in copies:
+            copy.wait_recv()
+        bands = left.at[:, c, pl.ds(h * band_half, band_half)]
+        return send(bands, bands, l_sib_ss.at[h], l_sib_rs.at[h], sibling)
+
+    l_copies, l_own = left_part(0)
 
     for copy in rs_copies[2:]:
         copy.wait_recv()
@@ -273,13 +286,7 @@
     for copy in r_copies:
         copy.wait_recv()
     r_sib = send(right.at[c], right.at[c], one_ss.at[0], one_rs.at[0], sibling)
-    l_own.wait()
-    for copy in l_copies:
-        copy.wait_recv()
-    l_sib = []
-    for j in range(nz):
-        band = left.at[aligned(2 * j + c, width)]
-        l_sib.append(send(band, band, l_sib_ss.at[j], l_sib_rs.at[j], sibling))
+    l_sib = [left_sibling(0, l_copies, l_own)]
 
     def rotate(r):
         at = aligned(lax.rem(x + CHUNKS - r, CHUNKS), size)
@@ -300,24 +307,29 @@
         g_sib.append(send(piece, piece, g_sib_ss.at[r], g_sib_rs.at[r], sibling))
         if r:
             rotate(r - 1)
+    l_copies_more, l_own = left_part(1)
     rotate(CHUNKS - 1)
 
-    for copy in l_sib:
-        copy.wait_recv()
-
-    @pl.loop(0, CHUNKS)
-    def _(r):
-        at = aligned(r, size)
-        eig[at] = dot(left[at], rot[...], ((1,), (0,))).astype(bf16)
+    def eigen(r):
+        at = aligned(r, band_size)
+        lhs = left[:, :, at, :].reshape(size, order)
+        out = dot(lhs, rot[...], ((1,), (0,))).astype(bf16)
+        eig[:, at, :] = out.reshape(2 * nz, band_size, nz * width)
         for i in range(1, nz):
             send(
-                eig.at[at, aligned(plus(i), width)],
-                ein.at[z, at],
+                eig.at[:, at, aligned(plus(i), width)],
+                ein.at[z, :, at],
                 e_ss.at[i, r],
                 e_rs.at[i, r],
                 peer(dp, plus(i)),
             )
-        local(eig.at[at, aligned(z, width)], ein.at[z, at], e_rs.at[0, r])
+        local(eig.at[:, at, aligned(z, width)], ein.at[z, :, at], e_rs.at[0, r])
+
+    l_sib[0].wait_recv()
+    pl.loop(0, CHUNKS // 2)(eigen)
+    l_sib.append(left_sibling(1, l_copies_more, l_own))
+    l_sib[1].wait_recv()
+    pl.loop(CHUNKS // 2, CHUNKS)(eigen)
 
     @pl.loop(0, CHUNKS)
     def _(r):
@@ -350,27 +362,27 @@
 
     @pl.loop(0, CHUNKS)
     def _(r):
-        at = aligned(r, size)
+        at = aligned(r, band_size)
         for i in list(range(1, nz)) + [0]:
             k = minus(i)
-            piece = ein.at[k, at]
+            piece = ein.at[k, :, at]
             pltpu.make_async_copy(piece, piece, e_rs.at[i, r]).wait()
-            e = ein[k, at].astype(f32)
-            new_first = first_beta * first[k, at] + (1.0 - first_beta) * e
-            new_second = second_beta * second[k, at] + (1.0 - second_beta) * e * e
-            first[k, at] = new_first
-            second[k, at] = new_second
-            nout[k, at] = (new_first / (jnp.sqrt(new_second) + epsilon)).astype(bf16)
+            e = ein[k, :, at].astype(f32)
+            new_first = first_beta * first[k, :, at] + (1.0 - first_beta) * e
+            new_second = second_beta * second[k, :, at] + (1.0 - second_beta) * e * e
+            first[k, :, at] = new_first
+            second[k, :, at] = new_second
+            nout[k, :, at] = (new_first / (jnp.sqrt(new_second) + epsilon)).astype(bf16)
             if i:
                 send(
-                    nout.at[k, at],
-                    normed.at[at, aligned(z, width)],
+                    nout.at[k, :, at],
+                    normed.at[:, at, aligned(z, width)],
                     n_ss.at[i, r],
                     n_rs.at[i, r],
                     peer(dp, k),
                 )
             else:
-                local(nout.at[k, at], normed.at[at, aligned(z, width)], n_rs.at[0, r])
+                local(nout.at[k, :, at], normed.at[:, at, aligned(z, width)], n_rs.at[0, r])
 
     def outer_send(out, into, ss, rs):
         copies = [
@@ -383,7 +395,7 @@
 
     for i in range(nz):
         for r in range(CHUNKS):
-            piece = normed.at[pl.ds(r * size, size), aligned(plus(i), width)]
+            piece = normed.at[:, pl.ds(r * band_size, band_size), aligned(plus(i), width)]
             pltpu.make_async_copy(piece, piece, n_rs.at[i, r]).wait()
 
     r_sib.wait_recv()
@@ -391,7 +403,9 @@
     @pl.loop(0, CHUNKS)
     def _(r):
         at = aligned(r, size)
-        back[c, at] = dot(left[:, at], normed[...], ((0,), (0,))).astype(bf16)
+        lhs = left[:, :, :, at].reshape(order, size)
+        rhs = normed[...].reshape(order, nz * width)
+        back[c, at] = dot(lhs, rhs, ((0,), (0,))).astype(bf16)
         send(back.at[c, at], back.at[c, at], b_sib_ss.at[r], b_sib_rs.at[r], sibling)
 
     for r in range(CHUNKS):
@@ -453,7 +467,7 @@
 
     factors(load_right, new_right, gtg_in, gt_own, gt_copies)
 
-    for copies in (r_copies, l_copies, rs_copies, l_sib, g_sib, [r_sib], gg_copies, gt_copies):
+    for copies in (r_copies, l_copies, l_copies_more, rs_copies, l_sib, g_sib, [r_sib], gg_copies, gt_copies):
         for copy in copies:
             copy.wait_send()
     for i in turns:
@@ -464,14 +478,34 @@
 
     @pl.loop(0, CHUNKS)
     def _(r):
-        at = aligned(r, size)
+        at, band = aligned(r, size), aligned(r, band_size)
         for i in range(1, nz):
-            piece = eig.at[at, aligned(plus(i), width)]
+            piece = eig.at[:, band, aligned(plus(i), width)]
             pltpu.make_async_copy(piece, piece, e_ss.at[i, r]).wait()
-            piece = nout.at[minus(i), at]
+            piece = nout.at[minus(i), :, band]
             pltpu.make_async_copy(piece, piece, n_ss.at[i, r]).wait()
         piece = back.at[c, at]
         pltpu.make_async_copy(piece, piece, b_sib_ss.at[r]).wait()
+
+
+def write_out(*refs):
+    count = len(refs) // 2
+    sems = refs[-1]
+    copies = []
+    for n in range(count):
+        for k in range(sems.shape[1]):
+            share = refs[n].shape[0] // sems.shape[1]
+            at = pl.ds(k * share, share)
+            copy = pltpu.make_async_copy(refs[n].at[at], refs[count + n].at[at], sems.at[n, k])
+            copy.start()
+            copies.append(copy)
+    for copy in copies:
+        copy.wait()
+
+
+def by_band(array):
+    slots, order, width = array.shape
+    return array.reshape(slots, order // width, width, width)
 
 
 def run_step(
@@ -482,15 +516,16 @@
     n_dp = lax.axis_size("dp")
     slots = n_dp * nz
     half = nz * width
-    large = (partial, left_basis, right_basis, left_factor, right_factor, first, second)
-    large = [pltpu.with_memory_space_constraint(array, pltpu.HBM) for array in large]
+    operands = (slot_of_block, partial, left_basis, right_basis)
+    operands += (left_factor, right_factor, by_band(first), by_band(second))
+    operands = [pltpu.with_memory_space_constraint(array, pltpu.HBM) for array in operands]
     vmem = pl.BlockSpec(memory_space=pltpu.VMEM)
-    smem = pl.BlockSpec(memory_space=pltpu.SMEM)
     hbm = pl.BlockSpec(memory_space=pltpu.HBM)
     dma = pltpu.SemaphoreType.DMA
     scratch = [
+        pltpu.SMEM(slot_of_block.shape, jnp.int32),
         pltpu.SMEM((slots,), jnp.int32),
-        pltpu.VMEM((nz, order, width), bf16),
+        pltpu.VMEM((nz, 2 * nz, width, width), bf16),
         pltpu.VMEM((nz, width, order), bf16),
         pltpu.VMEM((nz, width, order), bf16),
         pltpu.VMEM((nz, blocks, rows, width), bf16),
@@ -499,18 +534,18 @@
         pltpu.VMEM((blocks + 1, rows, width), bf16),
         pltpu.VMEM((slots, rows, width), bf16),
         pltpu.VMEM((2, order, half), bf16),
-        pltpu.VMEM((order, order), bf16),
+        pltpu.VMEM((nz, 2, width, order), bf16),
         pltpu.VMEM((2, order, half), bf16),
         pltpu.VMEM((order, half), bf16),
-        pltpu.VMEM((order, half), bf16),
-        pltpu.VMEM((nz, order, width), bf16),
-        pltpu.VMEM((order, half), bf16),
+        pltpu.VMEM((2 * nz, width, half), bf16),
+        pltpu.VMEM((nz, 2 * nz, width, width), bf16),
+        pltpu.VMEM((2 * nz, width, half), bf16),
         pltpu.VMEM((2, order, half), bf16),
         pltpu.VMEM((nz, width, order), bf16),
         pltpu.VMEM((nz, width, order), bf16),
         pltpu.VMEM((order, half), bf16),
         pltpu.VMEM((slots, rows, width), bf16),
-        dma((4,)),
+        dma((5,)),
         dma((nz,)),
         dma((nz,)),
         dma((nz,)),
@@ -520,8 +555,8 @@
         dma((CHUNKS + 1,)),
         dma((nz,)),
         dma((nz,)),
-        dma((nz,)),
-        dma((nz,)),
+        dma((2, nz)),
+        dma((2, nz)),
         dma((nz,)),
         dma((nz,)),
         dma((nz,)),
@@ -532,24 +567,24 @@
         dma((nz, CHUNKS)),
         dma((CHUNKS,)),
         dma((CHUNKS,)),
-        dma((nz,)),
-        dma((nz,)),
+        dma((2,)),
+        dma((2,)),
         dma((CHUNKS,)),
         dma((CHUNKS,)),
         dma((1,)),
         dma((1,)),
         pltpu.SemaphoreType.REGULAR((2,)),
     ]
-    return pl.pallas_call(
+    results = pl.pallas_call(
         functools.partial(step_kernel, n_dp, nz),
         out_shape=(
             jax.ShapeDtypeStruct((blocks, rows, width), bf16),
             jax.ShapeDtypeStruct((nz, width, order), f32),
             jax.ShapeDtypeStruct((nz, width, order), f32),
-            jax.ShapeDtypeStruct((nz, order, width), f32),
-            jax.ShapeDtypeStruct((nz, order, width), f32),
+            jax.ShapeDtypeStruct((nz, 2 * nz, width, width), f32),
+            jax.ShapeDtypeStruct((nz, 2 * nz, width, width), f32),
         ),
-        in_specs=[smem] + [hbm] * 7,
+        in_specs=[hbm] * 8,
         out_specs=(vmem,) * 5,
         scratch_shapes=scratch,
         compiler_params=pltpu.CompilerParams(
@@ -559,7 +594,17 @@
             flops=12 * order * order * half, bytes_accessed=16 * 2**20, transcendentals=0
         ),
         name="soap_step",
-    )(slot_of_block, *large)
+    )(*operands)
+    update, new_left, new_right, new_first, new_second = pl.pallas_call(
+        write_out,
+        out_shape=[jax.ShapeDtypeStruct(array.shape, array.dtype) for array in results],
+        in_specs=[pl.BlockSpec(memory_space=pl.ANY)] * 5,
+        out_specs=[hbm] * 5,
+        scratch_shapes=[dma((5, 4))],
+        compiler_params=pltpu.CompilerParams(vmem_limit_bytes=2**20),
+        name="write_out",
+    )(*results)
+    return update, new_left, new_right, new_first.reshape(first.shape), new_second.reshape(first.shape)
 
 
 def per_device(

time: 135 us -> 128 us (0.948)
  local copies, waits for them, and re-layouts: 6.72 us -> 0 us
    unnamed x7 -> x0, local copies, waits for them, and re-layouts: 6.72 us -> none
    pallas_call x0 -> x1, Pallas kernels: none -> 3.61 us  [run_step(): pl.pallas_call(write_out, out_shape=[jax.ShapeDtypeStruct(array.shape, ar...]
    pallas_call x1, Pallas kernels: 127 us -> 124 us  [run_step(): pl.pallas_call(functools.partial(step_kernel, n_dp, nz), out_shape=(jax.S...]
where the time goes in v4:
time: 128 us
  Pallas kernels  127 us (99%)
    pallas_call x1, Pallas kernels, run_step(): pl.pallas_call(functools.partial(step_kernel, n_dp, nz), out_shape=(jax.S...  124 us
    pallas_call x1, Pallas kernels, run_step(): pl.pallas_call(write_out, out_shape=[jax.ShapeDtypeStruct(array.shape, ar...  3.61 us

profile of v4, /device:TPU:1, one launch (start us, length us, event | category | flops | bytes accessed | tf_op | source)
XLA Modules:
  0.0 127.8 jit_solution(9647425957875169984)
XLA Ops:
  0.6 123.5 %soap_step.1 = (bf16[32,64,128]{2,1,0:T(8,128)(2,1)S(1)}, f32[4,128,1024]{2,1,0:T(8,128)S(1)}, f32[4,128,1024]{2,1,0:T(8,128)S(1)}, f32[4,8,128,128]{3,2,1,0:T(8,128)S(1)}, f32[4,8,128,128]{3,2,1,0:T(8,128)S(1)}) custom-call(s32[32]{0:T(128)} %slot_hbm.1, bf16[32,64,1024]{2,1,0:T(8,128)(2,1)} %bitcast.5, bf16[4,128,1024]{2,1,0:T(8,128)(2,1)} %lb.1, ...), custom_call_target="tpu_custom_call" | custom-call | flops 6442450944 | bytes 16777216 | tf_op jit(solution)/shard_map/soap_step/pallas_call | solution.py:578
  124.1 3.6 %write_out.1 = (bf16[32,64,128]{2,1,0:T(8,128)(2,1)}, f32[4,128,1024]{2,1,0:T(8,128)}, f32[4,128,1024]{2,1,0:T(8,128)}, f32[4,8,128,128]{3,2,1,0:T(8,128)}, f32[4,8,128,128]{3,2,1,0:T(8,128)}) custom-call(bf16[32,64,128]{2,1,0:T(8,128)(2,1)S(1)} %get-tuple-element.15.refs_0_, f32[4,128,1024]{2,1,0:T(8,128)S(1)} %get-tuple-element.16.refs_1_, ...), custom_call_target="tpu_custom_call" | custom-call | tf_op jit(solution)/shard_map/write_out/pallas_call | solution.py:598

commit v5 on v4

--- a/solution.py
+++ b/solution.py
@@ -94,7 +94,7 @@
     width = lb.shape[1]
     size = order // CHUNKS
     band_size = width // CHUNKS
-    band_half = width // 2
+    shares = (pl.ds(0, 3 * band_size), pl.ds(3 * band_size, band_size))
     dp = lax.axis_index("dp")
     t = lax.axis_index("tensor")
     z = t // 2
@@ -235,7 +235,7 @@
     load_right = local(right_hbm, new_right, load_sem.at[3])
 
     def left_part(h):
-        at = pl.ds(h * band_half, band_half)
+        at = shares[h]
         band = left.at[z, c, at]
         copies = [
             send(
@@ -249,7 +249,7 @@
         own.wait()
         for copy in copies:
             copy.wait_recv()
-        bands = left.at[:, c, pl.ds(h * band_half, band_half)]
+        bands = left.at[:, c, shares[h]]
         return send(bands, bands, l_sib_ss.at[h], l_sib_rs.at[h], sibling)
 
     l_copies, l_own = left_part(0)
@@ -326,10 +326,10 @@
         local(eig.at[:, at, aligned(z, width)], ein.at[z, :, at], e_rs.at[0, r])
 
     l_sib[0].wait_recv()
-    pl.loop(0, CHUNKS // 2)(eigen)
+    pl.loop(0, 3)(eigen)
     l_sib.append(left_sibling(1, l_copies_more, l_own))
     l_sib[1].wait_recv()
-    pl.loop(CHUNKS // 2, CHUNKS)(eigen)
+    pl.loop(3, CHUNKS)(eigen)
 
     @pl.loop(0, CHUNKS)
     def _(r):

time: 128 us -> 130 us (1.016)
  Pallas kernels: 127 us -> 129 us
    pallas_call x1, Pallas kernels: 124 us -> 125 us  [run_step(): pl.pallas_call(functools.partial(step_kernel, n_dp, nz), out_shape=(jax.S...]
where the time goes in v5:
time: 130 us; the launch traced here: 129 us
  Pallas kernels  129 us (99%)
    pallas_call x1, Pallas kernels, run_step(): pl.pallas_call(functools.partial(step_kernel, n_dp, nz), out_shape=(jax.S...  125 us
    pallas_call x1, Pallas kernels, run_step(): pl.pallas_call(write_out, out_shape=[jax.ShapeDtypeStruct(array.shape, ar...  3.61 us

profile of v5, /device:TPU:1, one launch (start us, length us, event | category | flops | bytes accessed | tf_op | source)
XLA Modules:
  0.0 129.4 jit_solution(2738670217510165513)
XLA Ops:
  0.6 125.2 %soap_step.1 = (bf16[32,64,128]{2,1,0:T(8,128)(2,1)S(1)}, f32[4,128,1024]{2,1,0:T(8,128)S(1)}, f32[4,128,1024]{2,1,0:T(8,128)S(1)}, f32[4,8,128,128]{3,2,1,0:T(8,128)S(1)}, f32[4,8,128,128]{3,2,1,0:T(8,128)S(1)}) custom-call(s32[32]{0:T(128)} %slot_hbm.1, bf16[32,64,1024]{2,1,0:T(8,128)(2,1)} %bitcast.5, bf16[4,128,1024]{2,1,0:T(8,128)(2,1)} %lb.1, ...), custom_call_target="tpu_custom_call" | custom-call | flops 6442450944 | bytes 16777216 | tf_op jit(solution)/shard_map/soap_step/pallas_call | solution.py:578
  125.8 3.6 %write_out.1 = (bf16[32,64,128]{2,1,0:T(8,128)(2,1)}, f32[4,128,1024]{2,1,0:T(8,128)}, f32[4,128,1024]{2,1,0:T(8,128)}, f32[4,8,128,128]{3,2,1,0:T(8,128)}, f32[4,8,128,128]{3,2,1,0:T(8,128)}) custom-call(bf16[32,64,128]{2,1,0:T(8,128)(2,1)S(1)} %get-tuple-element.15.refs_0_, f32[4,128,1024]{2,1,0:T(8,128)S(1)} %get-tuple-element.16.refs_1_, ...), custom_call_target="tpu_custom_call" | custom-call | tf_op jit(solution)/shard_map/write_out/pallas_call | solution.py:598
